TPU v7x, 128 devices: a whole 4x4x4 slice. The times are simulated.
128 devices in a mesh: region: 64 (over z, y, x), chan: 2 (over core).
Axes of the slice: x: 4, y: 4, z: 4, core: 2. Of those that a mesh axis runs over, the one named last changes fastest.
Arguments:
- patches: bfloat16 [4096, 8192], P('region', 'chan'), may hold values from -6 to 6
- patch_region: int32 [4096, 2], P('region'), may hold values from 0 to 63, all different within a row; in each aligned block of 64 rows (0 to 63, 64 to 127, ...) at most 4 rows name the same one
- patch_cell: int32 [4096, 2], P('region'), may hold values from 0 to 31
- w_first: bfloat16 [9, 128, 64], P(None, 'chan'), may hold values from -0.25 to 0.25
- w_down: bfloat16 [9, 256, 128], P(None, 'chan'), may hold values from -0.1875 to 0.1875
- w_deep: bfloat16 [9, 256, 256], P(None, 'chan'), may hold values from -0.125 to 0.125
- w_merge: bfloat16 [9, 128, 384], replicated, may hold values from -0.109375 to 0.109375
- w_out: bfloat16 [9, 64, 128], replicated, may hold values from -0.1875 to 0.1875
Outputs:
- downscaled: bfloat16 [64, 2048, 128], P('chan', 'region')
Inputs may be any that keep to these rules, and one draw needn't show every extreme that they name: `patch_region`: among the routes of the patches of one index of region, no region is named more than 4 times, a bound that some block reaches; a patch names 2 different regions.
All inputs are finite; a program needn't handle non-finite values.
Results may differ from a plain program's by a relative error of at most 0.013.
Values may be sent and summed in bfloat16 or wider, within the bound.
A program may use at most 64 MiB of HBM per device.

v0:
```python
import jax
import jax.numpy as jnp
from jax import lax
from jax.sharding import PartitionSpec as P

C0 = 64
C1 = 128
C2 = 256
TILE_H = 32
TILE_W = 128
PH = 8
PW = 16
BLOCKS = 32


def extended(cells, sides, width):
    for axis, dim in sides:
        count = lax.axis_size(axis)
        ends = count - 1
        head = lax.slice_in_dim(cells, 0, width, axis=dim)
        tail = lax.slice_in_dim(cells, cells.shape[dim] - width, cells.shape[dim], axis=dim)
        cells = jnp.concatenate(
            [
                lax.ppermute(tail, axis, [(i, (i + 1) % count) for i in range(ends)]),
                cells,
                lax.ppermute(head, axis, [((i + 1) % count, i) for i in range(ends)]),
            ],
            axis=dim,
        )
    return cells


def shifted(value, axis, steps):
    count = lax.axis_size(axis)
    initial, last = (max(0, -steps), min(count, count - steps))
    return lax.ppermute(value, axis, [(source, source + steps) for source in range(initial, last)])


def conv_taps(weights, padded_rows, stride, out_rows, out_cols):
    chans = padded_rows.shape[0]
    padded = jnp.pad(padded_rows, ((0, 0), (0, 0), (1, 1)))
    total = jnp.zeros((weights.shape[1], out_rows * out_cols), jnp.float32)
    for row_off in range(3):
        for col_off in range(3):
            window = lax.slice(
                padded,
                (0, row_off, col_off),
                (
                    chans,
                    row_off + stride * (out_rows - 1) + 1,
                    col_off + stride * (out_cols - 1) + 1,
                ),
                (1, stride, stride),
            )
            total = total + jnp.dot(
                weights[3 * row_off + col_off],
                window.reshape(chans, out_rows * out_cols),
                preferred_element_type=jnp.float32,
            )
    return total.reshape(weights.shape[1], out_rows, out_cols)


def spill_taps(weights, field):
    chans, height, width = field.shape
    padded = jnp.pad(field, ((0, 0), (0, 0), (1, 1)))
    total = jnp.zeros((weights.shape[1], height + 2, width), jnp.float32)
    for row_off in range(3):
        part = jnp.zeros((weights.shape[1], height * width), jnp.float32)
        for col_off in range(3):
            window = padded[:, :, col_off : col_off + width].reshape(chans, height * width)
            part = part + jnp.dot(
                weights[3 * row_off + col_off], window, preferred_element_type=jnp.float32
            )
        part = part.reshape(weights.shape[1], height, width)
        total = total + jnp.pad(part, ((0, 0), (2 - row_off, row_off), (0, 0)))
    return total


def with_rims(field):
    return extended(field, (("region", 1),), 1)


def encode(weights, haloed, stride, out_rows, out_cols):
    return conv_taps(
        weights, lax.all_gather(haloed, "chan", axis=0, tiled=True), stride, out_rows, out_cols
    )


def upsample_rims(haloed):
    rows_up = jnp.concatenate(
        [haloed[:, :1], jnp.repeat(haloed[:, 1:-1], 2, axis=1), haloed[:, -1:]], axis=1
    )
    return jnp.repeat(rows_up, 2, axis=2)


def shards(patches, patch_region, patch_cell, w_first, w_down, w_deep, w_merge, w_out):
    region_count = lax.axis_size("region")
    chan_count = lax.axis_size("chan")
    chan_index = lax.axis_index("chan")
    local_patches = patches.shape[0]
    intersection = patch_region.shape[1]
    slot_count = max(2, 2 * local_patches * intersection // region_count)
    route_count = local_patches * intersection
    targets = patch_region.reshape(route_count)
    cells = patch_cell.reshape(route_count)
    matches = (targets[:, None] == jnp.arange(region_count, dtype=jnp.int32)[None, :]).astype(
        jnp.int32
    )
    ranks = jnp.sum((jnp.cumsum(matches, axis=0) - matches) * matches, axis=1)
    slot_ids = targets * slot_count + ranks
    selector = slot_ids[None, :] == jnp.arange(region_count * slot_count, dtype=jnp.int32)[:, None]
    routed = jnp.repeat(patches, intersection, axis=0)
    payload = jnp.dot(
        selector.astype(jnp.bfloat16), routed, preferred_element_type=jnp.float32
    ).astype(jnp.bfloat16)
    payload = payload.reshape(region_count, slot_count, patches.shape[1])
    slot_cells = jnp.sum(jnp.where(selector, cells[None, :] + 1, 0), axis=1) - 1
    slot_cells = slot_cells.reshape(region_count, slot_count)
    arrived, arrived_cells = (
        lax.all_to_all(payload, "region", split_axis=0, concat_axis=0, tiled=True),
        lax.all_to_all(slot_cells, "region", split_axis=0, concat_axis=0, tiled=True),
    )
    placement = (
        arrived_cells.reshape(1, region_count * slot_count)
        == jnp.arange(BLOCKS, dtype=jnp.int32)[:, None]
    ).astype(jnp.bfloat16)
    summed = jnp.dot(
        placement,
        arrived.reshape(region_count * slot_count, patches.shape[1]),
        preferred_element_type=jnp.float32,
    ).astype(jnp.bfloat16)
    local_in = C0 // chan_count
    inputs = (
        summed.reshape(TILE_H // PH, TILE_W // PW, local_in, PH, PW)
        .transpose(2, 0, 3, 1, 4)
        .reshape(local_in, TILE_H, TILE_W)
    )
    first = jax.nn.silu(encode(w_first, with_rims(inputs), 1, TILE_H, TILE_W)).astype(jnp.bfloat16)
    halo_first = with_rims(first)
    down_sum = encode(w_down, halo_first, 2, TILE_H // 2, TILE_W // 2)
    second = jax.nn.silu(down_sum).astype(jnp.bfloat16)
    third = (
        jax.nn.silu(encode(w_deep, with_rims(second), 1, TILE_H // 2, TILE_W // 2))
        + second.astype(jnp.float32)
    ).astype(jnp.bfloat16)
    halo_third = with_rims(third)
    out_share = C1 // chan_count
    first_share = C1 // chan_count
    second_share = C2 // chan_count
    joined = jnp.concatenate([halo_first, upsample_rims(halo_third)], axis=0)
    own_rows = lax.dynamic_slice_in_dim(w_merge, chan_index * out_share, out_share, 1)
    skip_part = own_rows[:, :, :C1].reshape(9, out_share, chan_count, first_share)
    deep_part = own_rows[:, :, C1:].reshape(9, out_share, chan_count, second_share)
    ordered = jnp.concatenate([skip_part, deep_part], axis=3).reshape(9, out_share, C1 + C2)
    merged = conv_taps(
        ordered, lax.all_gather(joined, "chan", axis=0, tiled=True), 1, TILE_H, TILE_W
    )
    fourth = jax.nn.silu(merged).astype(jnp.bfloat16)
    own_out = lax.dynamic_slice_in_dim(w_out, chan_index * first_share, first_share, 2)
    spilled = lax.psum_scatter(
        spill_taps(own_out, fourth).astype(jnp.bfloat16), "chan", scatter_dimension=0, tiled=True
    ).astype(jnp.float32)
    from_above = shifted(spilled[:, TILE_H + 1 :], "region", 1)
    from_below = shifted(spilled[:, :1], "region", -1)
    correction = (
        spilled[:, 1 : TILE_H + 1]
        + jnp.pad(from_above, ((0, 0), (0, TILE_H - 1), (0, 0)))
        + jnp.pad(from_below, ((0, 0), (TILE_H - 1, 0), (0, 0)))
    )
    return (inputs.astype(jnp.float32) + correction).astype(jnp.bfloat16)


def solution(mesh):
    placed = (
        P("region", "chan"),
        P("region", None),
        P("region", None),
        P(None, "chan", None),
        P(None, "chan", None),
        P(None, "chan", None),
        P(),
        P(),
    )
    return jax.shard_map(
        shards, mesh=mesh, in_specs=placed, out_specs=P("chan", "region", None), check_vma=False
    )
```

profile of v0, /device:TPU:1, one launch (start us, length us, event | category | flops | bytes accessed | tf_op | source)
XLA Modules:
  0.0 282.2 jit_solution(8030164357141075776)
XLA Ops:
  6.5 0.8 copy.100
  9.8 12.0 %all-to-all-start = ((s32[64,1,4]{2,1,0:T(1,128)}), s32[64,1,4]{2,1,0:T(1,128)S(1)}, u32[]{:S(2)}, u32[]{:S(2)}) async-start(s32[64,1,4]{2,1,0:T(1,128)} %bitcast), calls=%async_computation | async-start | bytes 65536 | tf_op jit(solution)/shard_map/all_to_all | solution.py:121
  21.7 2.0 broadcast_in_dim.27
  23.8 1.2 reshape.229
  25.0 1.9 convolution_convert_fusion
  26.9 2.2 reshape.230
  29.2 0.9 all-to-all-done
  30.1 8.9 %all-to-all-start.1 = ((bf16[64,4,4096]{2,1,0:T(4,128)(2,1)}), bf16[64,4,4096]{2,1,0:T(4,128)(2,1)S(1)}, u32[]{:S(2)}, u32[]{:S(2)}) async-start(bf16[64,4,4096]{2,1,0:T(4,128)(2,1)} %reshape.230), calls=%async_computation.1 | async-start | bytes 4194304 | tf_op jit(solution)/shard_map/all_to_all | solution.py:120
  40.4 26.7 %all-to-all-done.1 = bf16[64,4,4096]{2,1,0:T(4,128)(2,1)S(1)} async-done(((bf16[64,4,4096]{2,1,0:T(4,128)(2,1)}), bf16[64,4,4096]{2,1,0:T(4,128)(2,1)S(1)}, u32[]{:S(2)}, u32[]{:S(2)}) %all-to-all-start.1) | async-done | bytes 2097184 | tf_op jit(solution)/shard_map/all_to_all | solution.py:120
  67.1 2.0 reshape.231
  69.1 2.0 convolution_convert_fusion.1
  71.2 2.7 reshape.232
  73.8 2.4 copy.103
  76.3 2.3 collective-permute-start
  78.5 1.3 collective-permute-start.1
  80.3 2.9 %collective-permute-done.1 = bf16[32,1,128]{0,2,1:T(8,128)(2,1)S(1)} collective-permute-done((bf16[32,1,128]{0,2,1:T(8,128)(2,1)S(1)}, bf16[32,1,128]{0,2,1:T(8,128)(2,1)S(1)}, u32[]{:S(2)}, u32[]{:S(2)}) %collective-permute-start.1) | collective-permute-done | bytes 8224 | tf_op jit(solution)/shard_map/ppermute | solution.py:26
  83.3 6.0 %all_gather.12 = bf16[64,34,128]{2,0,1:T(8,128)(2,1)S(1)} all-gather(bf16[32,34,128]{2,0,1:T(8,128)(2,1)S(1)} %pad_maximum_fusion.4), channel_id=1, replica_groups=mesh['region'=64,'chan'=2] {'chan'}, dimensions={0}, use_global_device_ids=true | all-gather | bytes 835584 | tf_op jit(solution)/shard_map/all_gather | solution.py:85
  89.3 1.2 fusion.20
  93.7 2.5 collective-permute-start.2
  96.1 1.3 collective-permute-start.3
  97.5 3.3 %collective-permute-done.3 = bf16[64,1,128]{2,1,0:T(2,128)(2,1)S(1)} collective-permute-done((bf16[64,1,128]{2,1,0:T(2,128)(2,1)S(1)}, bf16[64,1,128]{2,1,0:T(2,128)(2,1)S(1)}, u32[]{:S(2)}, u32[]{:S(2)}) %collective-permute-start.3) | collective-permute-done | bytes 16416 | tf_op jit(solution)/shard_map/ppermute | solution.py:26
  101.1 0.9 copy.116
  102.3 20.0 %all-gather.3.cloned.1.call-done = bf16[128,34,128]{2,0,1:T(8,128)(2,1)} async-done(((bf16[64,34,128]{2,0,1:T(8,128)(2,1)}), bf16[128,34,128]{2,0,1:T(8,128)(2,1)}) %all-gather.3.cloned.1.call-update) | async-done | bytes 1114128 | tf_op jit(solution)/shard_map/all_gather | solution.py:85
  122.4 2.4 copy.117
  124.7 1.6 pad.41
  126.9 5.0 %slice.341 = bf16[128,16,64]{0,2,1:T(8,128)(2,1)} slice(bf16[128,34,130]{0,2,1:T(8,128)(2,1)S(1)} %pad.41), slice={[0:128:1], [0:31:2], [1:128:2]} | slice | bytes 524288 | tf_op jit(solution)/shard_map/slice | solution.py:45
  132.0 5.0 %slice.343 = bf16[128,16,64]{0,2,1:T(8,128)(2,1)} slice(bf16[128,34,130]{0,2,1:T(8,128)(2,1)S(1)} %pad.41), slice={[0:128:1], [0:31:2], [2:129:2]} | slice | bytes 524288 | tf_op jit(solution)/shard_map/slice | solution.py:45
  136.9 5.0 %slice.345 = bf16[128,16,64]{0,2,1:T(8,128)(2,1)} slice(bf16[128,34,130]{0,2,1:T(8,128)(2,1)S(1)} %pad.41), slice={[0:128:1], [1:32:2], [0:127:2]} | slice | bytes 524288 | tf_op jit(solution)/shard_map/slice | solution.py:45
  141.9 5.0 %slice.347 = bf16[128,16,64]{0,2,1:T(8,128)(2,1)} slice(bf16[128,34,130]{0,2,1:T(8,128)(2,1)S(1)} %pad.41), slice={[0:128:1], [1:32:2], [1:128:2]} | slice | bytes 524288 | tf_op jit(solution)/shard_map/slice | solution.py:45
  146.9 5.0 %slice.349 = bf16[128,16,64]{0,2,1:T(8,128)(2,1)} slice(bf16[128,34,130]{0,2,1:T(8,128)(2,1)S(1)} %pad.41), slice={[0:128:1], [1:32:2], [2:129:2]} | slice | bytes 524288 | tf_op jit(solution)/shard_map/slice | solution.py:45
  151.9 5.0 %slice.351 = bf16[128,16,64]{0,2,1:T(8,128)(2,1)} slice(bf16[128,34,130]{0,2,1:T(8,128)(2,1)S(1)} %pad.41), slice={[0:128:1], [2:33:2], [0:127:2]} | slice | bytes 524288 | tf_op jit(solution)/shard_map/slice | solution.py:45
  158.0 1.1 fusion.84
  159.1 1.2 convolution_add_fusion.29
  160.3 1.2 convolution_add_fusion.28
  163.1 3.2 %collective-permute-start.4 = (bf16[128,1,64]{0,2,1:T(8,128)(2,1)S(1)}, bf16[128,1,64]{0,2,1:T(8,128)(2,1)S(1)}, u32[]{:S(2)}, u32[]{:S(2)}) collective-permute-start(bf16[128,1,64]{0,2,1:T(8,128)(2,1)S(1)} %get-tuple-element.50), channel_id=1, source_target_pairs={{0,2},{2,4},{4,6},{6,8},{8,10},{10,12},{12,14},{14,16},{16,18},{18... | collective-permute-start | bytes 49160 | tf_op jit(solution)/shard_map/ppermute | solution.py:24
  166.3 1.3 collective-permute-start.5
  167.6 3.2 %collective-permute-done.5 = bf16[128,1,64]{0,2,1:T(8,128)(2,1)S(1)} collective-permute-done((bf16[128,1,64]{0,2,1:T(8,128)(2,1)S(1)}, bf16[128,1,64]{0,2,1:T(8,128)(2,1)S(1)}, u32[]{:S(2)}, u32[]{:S(2)}) %collective-permute-start.5) | collective-permute-done | bytes 16416 | tf_op jit(solution)/shard_map/ppermute | solution.py:26
  170.8 3.5 %all_gather.14 = bf16[256,18,64]{0,2,1:T(8,128)(2,1)S(1)} all-gather(bf16[128,18,64]{0,2,1:T(8,128)(2,1)S(1)} %pad_maximum_fusion.3), channel_id=1, replica_groups=mesh['region'=64,'chan'=2] {'chan'}, dimensions={0}, use_global_device_ids=true | all-gather | bytes 884736 | tf_op jit(solution)/shard_map/all_gather | solution.py:85
  178.4 3.0 %collective-permute-start.6 = (bf16[128,1,64]{0,2,1:T(8,128)(2,1)S(1)}, bf16[128,1,64]{0,2,1:T(8,128)(2,1)S(1)}, u32[]{:S(2)}, u32[]{:S(2)}) collective-permute-start(bf16[128,1,64]{0,2,1:T(8,128)(2,1)S(1)} %get-tuple-element.48), channel_id=1, source_target_pairs={{0,2},{2,4},{4,6},{6,8},{8,10},{10,12},{12,14},{14,16},{16,18},{18... | collective-permute-start | bytes 49160 | tf_op jit(solution)/shard_map/ppermute | solution.py:24
  181.5 1.3 collective-permute-start.7
  182.8 1.5 copy.118
  184.3 1.6 collective-permute-done.7
  187.0 1.0 pad_maximum_fusion
  188.0 2.3 copy.119
  190.7 1.0 slice_maximum_fusion
  195.9 18.7 %all-gather.5.cloned.1.call-done = bf16[384,34,128]{2,0,1:T(8,128)(2,1)} async-done(((bf16[192,34,128]{2,0,1:T(8,128)(2,1)}), bf16[384,34,128]{2,0,1:T(8,128)(2,1)}) %all-gather.5.cloned.1.call-update) | async-done | bytes 3342352 | tf_op jit(solution)/shard_map/all_gather | solution.py:156
  214.6 5.6 %copy.120 = bf16[384,34,128]{0,2,1:T(8,128)(2,1)S(1)} copy(bf16[384,34,128]{2,0,1:T(8,128)(2,1)} %all-gather.5.cloned.1.call-done) | data formatting | bytes 6684672 | tf_op jit(solution)/shard_map/all_gather | solution.py:156
  220.2 11.5 %pad_slice_fusion = (bf16[384,32,128]{0,2,1:T(8,128)(2,1)S(1)}, bf16[384,32,128]{0,2,1:T(8,128)(2,1)}, bf16[384,32,128]{0,2,1:T(8,128)(2,1)}, bf16[384,32,128]{0...) fusion(bf16[384,34,128]{0,2,1:T(8,128)(2,1)S(1)} %copy.120), kind=kLoop, calls=%fused_computation.29 | loop fusion | bytes 41091072 | tf_op jit(solution)/shard_map/slice | solution.py:45
  231.8 3.1 %fusion.128 = f32[64,4096]{1,0:T(8,128)S(1)} fusion(bf16[64,384]{1,0:T(8,128)(2,1)S(1)} %copy-done.19, bf16[384,4096]{0,1:T(8,128)(2,1)} %bitcast.292), kind=kOutput, calls=%fused_computation.233 | convolution fusion | flops 201326592 | bytes 4243456 | tf_op jit(solution)/shard_map/dot_general | solution.py:55
  235.0 1.1 convolution_add_fusion.21
  236.8 1.1 convolution_add_fusion.20
  238.2 1.1 convolution_add_fusion.19
  239.9 1.1 convolution_add_fusion.18
  241.0 1.1 convolution_add_fusion.17
  242.1 1.1 convolution_add_fusion.16
  243.3 1.1 convolution_add_fusion.15
  244.4 1.1 convolution_add_fusion.14
  250.7 1.3 add_convert_fusion
  252.0 12.3 %reduce-scatter.2.cloned.1.call-done = bf16[32,34,128]{2,1,0:T(8,128)(2,1)} async-done(((bf16[64,34,128]{2,1,0:T(8,128)(2,1)}), bf16[32,34,128]{2,1,0:T(8,128)(2,1)}) %reduce-scatter.2.cloned.1.call-update) | async-done | bytes 278544 | tf_op jit(solution)/shard_map/reduce_scatter | solution.py:160
  264.3 1.5 copy.124
  265.8 3.2 %collective-permute-start.8 = (f32[32,1,128]{0,2,1:T(8,128)S(1)}, f32[32,1,128]{0,2,1:T(8,128)S(1)}, u32[]{:S(2)}, u32[]{:S(2)}) collective-permute-start(f32[32,1,128]{0,2,1:T(8,128)S(1)} %get-tuple-element.22), channel_id=1, source_target_pairs={{0,2},{2,4},{4,6},{6,8},{8,10},{10,12},{12,14},{14,16},{16,18},{18... | collective-permute-start | bytes 49160 | tf_op jit(solution)/shard_map/ppermute | solution.py:36
  269.0 1.3 collective-permute-start.9
  270.6 3.4 %collective-permute-done.9 = f32[32,1,128]{0,2,1:T(8,128)S(1)} collective-permute-done((f32[32,1,128]{0,2,1:T(8,128)S(1)}, f32[32,1,128]{0,2,1:T(8,128)S(1)}, u32[]{:S(2)}, u32[]{:S(2)}) %collective-permute-start.9) | collective-permute-done | bytes 16416 | tf_op jit(solution)/shard_map/ppermute | solution.py:36
  274.4 1.2 copy.125
  (146 shorter events, 27.9 us)
Async XLA Ops:
  6.5 183.9 %copy-start = (bf16[9,128,384]{2,1,0:T(8,128)(2,1)S(1)}, bf16[9,128,384]{2,1,0:T(8,128)(2,1)}, u32[]{:S(2)}) copy-start(bf16[9,128,384]{2,1,0:T(8,128)(2,1)} %param.14) | copy-start | bytes 2654212
  9.8 20.3 %all-to-all-start = ((s32[64,1,4]{2,1,0:T(1,128)}), s32[64,1,4]{2,1,0:T(1,128)S(1)}, u32[]{:S(2)}, u32[]{:S(2)}) async-start(s32[64,1,4]{2,1,0:T(1,128)} %bitcast), calls=%async_computation | async-start | bytes 65536 | tf_op jit(solution)/shard_map/all_to_all | solution.py:121
  30.1 37.0 %all-to-all-start.1 = ((bf16[64,4,4096]{2,1,0:T(4,128)(2,1)}), bf16[64,4,4096]{2,1,0:T(4,128)(2,1)S(1)}, u32[]{:S(2)}, u32[]{:S(2)}) async-start(bf16[64,4,4096]{2,1,0:T(4,128)(2,1)} %reshape.230), calls=%async_computation.1 | async-start | bytes 4194304 | tf_op jit(solution)/shard_map/all_to_all | solution.py:120
  39.0 83.4 %all-gather.3.cloned.1.call-start = ((), (), s32[]{:S(2)}) async-start(), calls=%async_computation.3 | async-start | bytes 1671168 | tf_op jit(solution)/shard_map/all_gather | solution.py:85
  76.3 14.3 %copy-start.6 = (bf16[32,4,8,8,16]{0,4,3,2,1:T(8,128)(2,1)}, bf16[32,4,8,8,16]{0,4,3,2,1:T(8,128)(2,1)S(1)}, u32[]{:S(2)}) copy-start(bf16[32,4,8,8,16]{0,4,3,2,1:T(8,128)(2,1)S(1)} %copy.103) | copy-start | bytes 786436
  76.3 3.9 %collective-permute-start = (bf16[32,1,128]{0,2,1:T(8,128)(2,1)S(1)}, bf16[32,1,128]{0,2,1:T(8,128)(2,1)S(1)}, u32[]{:S(2)}, u32[]{:S(2)}) collective-permute-start(bf16[32,1,128]{0,2,1:T(8,128)(2,1)S(1)} %get-tuple-element.24), channel_id=1, source_target_pairs={{0,2},{2,4},{4,6},{6,8},{8,10},{10,12},{12,14},{14,16},{16,18},{18... | collective-permute-start | bytes 24584 | tf_op jit(solution)/shard_map/ppermute | solution.py:24
  78.5 4.7 %collective-permute-start.1 = (bf16[32,1,128]{0,2,1:T(8,128)(2,1)S(1)}, bf16[32,1,128]{0,2,1:T(8,128)(2,1)S(1)}, u32[]{:S(2)}, u32[]{:S(2)}) collective-permute-start(bf16[32,1,128]{0,2,1:T(8,128)(2,1)S(1)} %get-tuple-element.25), channel_id=1, source_target_pairs={{2,0},{4,2},{6,4},{8,6},{10,8},{12,10},{14,12},{16,14},{18,16},{20... | collective-permute-start | bytes 24584 | tf_op jit(solution)/shard_map/ppermute | solution.py:26
  89.3 1.2 copy-start.20
  93.7 3.8 %collective-permute-start.2 = (bf16[64,1,128]{2,1,0:T(2,128)(2,1)S(1)}, bf16[64,1,128]{2,1,0:T(2,128)(2,1)S(1)}, u32[]{:S(2)}, u32[]{:S(2)}) collective-permute-start(bf16[64,1,128]{2,1,0:T(2,128)(2,1)S(1)} %get-tuple-element.46), channel_id=1, source_target_pairs={{0,2},{2,4},{4,6},{6,8},{8,10},{10,12},{12,14},{14,16},{16,18},{18... | collective-permute-start | bytes 49160 | tf_op jit(solution)/shard_map/ppermute | solution.py:24
  96.1 4.7 %collective-permute-start.3 = (bf16[64,1,128]{2,1,0:T(2,128)(2,1)S(1)}, bf16[64,1,128]{2,1,0:T(2,128)(2,1)S(1)}, u32[]{:S(2)}, u32[]{:S(2)}) collective-permute-start(bf16[64,1,128]{2,1,0:T(2,128)(2,1)S(1)} %get-tuple-element.47), channel_id=1, source_target_pairs={{2,0},{4,2},{6,4},{8,6},{10,8},{12,10},{14,12},{16,14},{18,16},{20... | collective-permute-start | bytes 49160 | tf_op jit(solution)/shard_map/ppermute | solution.py:26
  102.1 112.5 %all-gather.5.cloned.1.call-start = ((), (), s32[]{:S(2)}) async-start(), calls=%async_computation.4 | async-start | bytes 5013504 | tf_op jit(solution)/shard_map/all_gather | solution.py:156
  158.0 3.5 %copy-start.12 = (bf16[128,16,64]{0,2,1:T(8,128)(2,1)S(1)}, bf16[128,16,64]{0,2,1:T(8,128)(2,1)}, u32[]{:S(2)}) copy-start(bf16[128,16,64]{0,2,1:T(8,128)(2,1)} %slice.345) | copy-start | bytes 786436
  158.0 3.5 %copy-start.14 = (bf16[9,128,128]{2,1,0:T(8,128)(2,1)S(1)}, bf16[9,128,128]{2,1,0:T(8,128)(2,1)}, u32[]{:S(2)}) copy-start(bf16[9,128,128]{2,1,0:T(8,128)(2,1)} %param.12) | copy-start | bytes 884740
  158.0 3.8 %copy-start.11 = (bf16[128,16,64]{0,2,1:T(8,128)(2,1)S(1)}, bf16[128,16,64]{0,2,1:T(8,128)(2,1)}, u32[]{:S(2)}) copy-start(bf16[128,16,64]{0,2,1:T(8,128)(2,1)} %slice.347) | copy-start | bytes 786436
  158.0 4.0 %copy-start.10 = (bf16[128,16,64]{0,2,1:T(8,128)(2,1)S(1)}, bf16[128,16,64]{0,2,1:T(8,128)(2,1)}, u32[]{:S(2)}) copy-start(bf16[128,16,64]{0,2,1:T(8,128)(2,1)} %slice.349) | copy-start | bytes 786436
  159.1 3.2 %copy-start.9 = (bf16[128,16,64]{0,2,1:T(8,128)(2,1)S(1)}, bf16[128,16,64]{0,2,1:T(8,128)(2,1)}, u32[]{:S(2)}) copy-start(bf16[128,16,64]{0,2,1:T(8,128)(2,1)} %slice.351) | copy-start | bytes 786436
  163.1 4.5 %collective-permute-start.4 = (bf16[128,1,64]{0,2,1:T(8,128)(2,1)S(1)}, bf16[128,1,64]{0,2,1:T(8,128)(2,1)S(1)}, u32[]{:S(2)}, u32[]{:S(2)}) collective-permute-start(bf16[128,1,64]{0,2,1:T(8,128)(2,1)S(1)} %get-tuple-element.50), channel_id=1, source_target_pairs={{0,2},{2,4},{4,6},{6,8},{8,10},{10,12},{12,14},{14,16},{16,18},{18... | collective-permute-start | bytes 49160 | tf_op jit(solution)/shard_map/ppermute | solution.py:24
  166.3 4.5 %collective-permute-start.5 = (bf16[128,1,64]{0,2,1:T(8,128)(2,1)S(1)}, bf16[128,1,64]{0,2,1:T(8,128)(2,1)S(1)}, u32[]{:S(2)}, u32[]{:S(2)}) collective-permute-start(bf16[128,1,64]{0,2,1:T(8,128)(2,1)S(1)} %get-tuple-element.51), channel_id=1, source_target_pairs={{2,0},{4,2},{6,4},{8,6},{10,8},{12,10},{14,12},{16,14},{18,16},{20... | collective-permute-start | bytes 49160 | tf_op jit(solution)/shard_map/ppermute | solution.py:26
  174.3 1.1 copy-start.13
  178.4 5.9 %collective-permute-start.6 = (bf16[128,1,64]{0,2,1:T(8,128)(2,1)S(1)}, bf16[128,1,64]{0,2,1:T(8,128)(2,1)S(1)}, u32[]{:S(2)}, u32[]{:S(2)}) collective-permute-start(bf16[128,1,64]{0,2,1:T(8,128)(2,1)S(1)} %get-tuple-element.48), channel_id=1, source_target_pairs={{0,2},{2,4},{4,6},{6,8},{8,10},{10,12},{12,14},{14,16},{16,18},{18... | collective-permute-start | bytes 49160 | tf_op jit(solution)/shard_map/ppermute | solution.py:24
  181.5 4.5 %collective-permute-start.7 = (bf16[128,1,64]{0,2,1:T(8,128)(2,1)S(1)}, bf16[128,1,64]{0,2,1:T(8,128)(2,1)S(1)}, u32[]{:S(2)}, u32[]{:S(2)}) collective-permute-start(bf16[128,1,64]{0,2,1:T(8,128)(2,1)S(1)} %get-tuple-element.49), channel_id=1, source_target_pairs={{2,0},{4,2},{6,4},{8,6},{10,8},{12,10},{14,12},{16,14},{18,16},{20... | collective-permute-start | bytes 49160 | tf_op jit(solution)/shard_map/ppermute | solution.py:26
  184.3 2.7 copy-start.8
  190.3 74.0 %reduce-scatter.2.cloned.1.call-start = ((), (), s32[]{:S(2)}) async-start(), calls=%async_computation.5 | async-start | bytes 983040 | tf_op jit(solution)/shard_map/reduce_scatter | solution.py:160
  220.2 11.6 %copy-start.19 = (bf16[64,384]{1,0:T(8,128)(2,1)S(1)}, bf16[64,384]{1,0:T(8,128)(2,1)}, u32[]{:S(2)}) copy-start(bf16[64,384]{1,0:T(8,128)(2,1)} %squeeze.136) | copy-start | bytes 147460
  231.8 3.2 %copy-start.5 = (bf16[384,32,128]{0,2,1:T(8,128)(2,1)S(1)}, bf16[384,32,128]{0,2,1:T(8,128)(2,1)}, u32[]{:S(2)}) copy-start(bf16[384,32,128]{0,2,1:T(8,128)(2,1)} %get-tuple-element.12) | copy-start | bytes 9437188
  231.8 3.2 %copy-start.18 = (bf16[64,384]{1,0:T(8,128)(2,1)S(1)}, bf16[64,384]{1,0:T(8,128)(2,1)}, u32[]{:S(2)}) copy-start(bf16[64,384]{1,0:T(8,128)(2,1)} %squeeze.164) | copy-start | bytes 147460
  234.9 1.9 copy-start.4
  235.0 1.9 copy-start.17
  236.1 2.1 copy-start.3
  236.1 2.1 copy-start.16
  238.0 1.9 copy-start.2
  238.0 1.9 copy-start.15
  245.5 0.9 copy-start.21
  252.0 22.1 %copy-start.7 = (bf16[32,4,8,8,16]{0,4,3,2,1:T(8,128)(2,1)S(1)}, bf16[32,4,8,8,16]{0,4,3,2,1:T(8,128)(2,1)}, u32[]{:S(2)}) copy-start(bf16[32,4,8,8,16]{0,4,3,2,1:T(8,128)(2,1)} %copy-done.6) | copy-start | bytes 786436
  265.8 4.8 %collective-permute-start.8 = (f32[32,1,128]{0,2,1:T(8,128)S(1)}, f32[32,1,128]{0,2,1:T(8,128)S(1)}, u32[]{:S(2)}, u32[]{:S(2)}) collective-permute-start(f32[32,1,128]{0,2,1:T(8,128)S(1)} %get-tuple-element.22), channel_id=1, source_target_pairs={{0,2},{2,4},{4,6},{6,8},{8,10},{10,12},{12,14},{14,16},{16,18},{18... | collective-permute-start | bytes 49160 | tf_op jit(solution)/shard_map/ppermute | solution.py:36
  269.0 5.0 %collective-permute-start.9 = (f32[32,1,128]{0,2,1:T(8,128)S(1)}, f32[32,1,128]{0,2,1:T(8,128)S(1)}, u32[]{:S(2)}, u32[]{:S(2)}) collective-permute-start(f32[32,1,128]{0,2,1:T(8,128)S(1)} %get-tuple-element.23), channel_id=1, source_target_pairs={{2,0},{4,2},{6,4},{8,6},{10,8},{12,10},{14,12},{16,14},{18,16},{20... | collective-permute-start | bytes 49160 | tf_op jit(solution)/shard_map/ppermute | solution.py:36
  270.3 5.3 %copy-start.1 = (bf16[9,128,384]{2,1,0:T(8,128)(2,1)S(1)}, bf16[9,128,384]{2,1,0:T(8,128)(2,1)}, u32[]{:S(2)}) copy-start(bf16[9,128,384]{2,1,0:T(8,128)(2,1)} %param.14) | copy-start | bytes 2654212
Sparse Core Ops, SparseCore 0:
  102.2 20.1 all-gather.2
  190.5 24.0 all-gather.4
  252.1 12.1 reduce-scatter.1
where the time goes:
time: 287 us; the launch traced here: 282 us
  waiting for transfers between devices  93.3 us (33%)
  local copies, waits for them, and re-layouts  86.4 us (30%)
  starting transfers between devices  41.8 us (15%)
  matrix products  29.6 us (10%)
  between operations  14.1 us (5%)
  blocking collectives  9.52 us (3%)
  other arithmetic  7.53 us (3%)
    slice x11, local copies, waits for them, and re-layouts, conv_taps(): lax.slice(padded, (0, row_off, col_off), (chans, row_off + stride * (out_...  43.8 us
    all_to_all x1, waiting for transfers between devices, shards(): lax.all_to_all(payload, 'region', split_axis=0, concat_axis=0, tiled=True)  26.7 us
    dot_general x36, matrix products, conv_taps(): jnp.dot(weights[3 * row_off + col_off], window.reshape(chans, out_rows *...  22 us
    all_gather x1, waiting for transfers between devices, encode(): lax.all_gather(haloed, 'chan', axis=0, tiled=True)  20 us
    all_gather x1, waiting for transfers between devices, shards(): lax.all_gather(joined, 'chan', axis=0, tiled=True)  18.7 us
    reduce_scatter x1, waiting for transfers between devices, shards(): lax.psum_scatter(spill_taps(own_out, fourth).astype(jnp.bfloat16), 'chan'...  12.3 us
    all_to_all x1, starting transfers between devices, shards(): lax.all_to_all(slot_cells, 'region', split_axis=0, concat_axis=0, tiled=T...  12 us
    ppermute x4, waiting for transfers between devices, extended(): lax.ppermute(head, axis, [((i + 1) % count, i) for i in range(ends)])  11.1 us
  transfers between devices with their start and end apart: 15, of which 10 were waited for; matrix products, arithmetic and copies ran while one was open for 6% of the time, Pallas kernels for 0%

commit v1 on v0

v1 whole, which is shorter than its diff:
```python
import jax
import jax.numpy as jnp
from jax import lax
from jax.experimental import pallas as pl
from jax.experimental.pallas import tpu as pltpu
from jax.sharding import PartitionSpec as P

C0 = 64
C1 = 128
C2 = 256
W = 128
HALF = 16
F32 = jnp.float32
BF16 = jnp.bfloat16
MESH = pl.DeviceIdType.MESH

OFFSETS = sorted(
    range(1, 64),
    key=lambda g: (-sum(min(v, 4 - v) for v in (g // 16, (g // 4) % 4, g % 4)), (g * 37) % 64),
)


def iota(shape, axis):
    return lax.broadcasted_iota(jnp.int32, shape, axis)


def shift(x, step):
    lane = iota(x.shape, 1)
    keep = lane < W - step if step > 0 else lane >= -step
    return jnp.where(keep, pltpu.roll(x, (-step) % W, 1), 0.0)


def silu(v):
    h = 0.5 * v
    return h + h * jnp.tanh(h)


def swap_granules(x):
    rows = x.shape[0]
    row, gran = iota(x.shape, 0), iota(x.shape, 1) // 16
    for s in (1, 2, 4):
        down = pltpu.roll(pltpu.roll(x, 16 * s, 1), rows - s, 0)
        up = pltpu.roll(pltpu.roll(x, W - 16 * s, 1), s, 0)
        row_bit, gran_bit = (row & s) != 0, (gran & s) != 0
        x = jnp.where(row_bit == gran_bit, x, jnp.where(gran_bit, down, up))
    return x


def kernel(
    patches_ref, region_ref, cell_ref, wf_ref, wd_ref, wp_ref, wm_ref, wo_ref,
    out_ref,
    payload, arrived, cells_out, cells_in,
    wf, wd, wp, wm, wo,
    place, grid_f, grid_own, grid, im1, im2, imd, im4, out_f, out_b,
    a2a_send, a2a_recv, cell_send, cell_recv, w_send, w_recv, g_send, g_recv, o_send, o_recv,
):
    r, c = lax.axis_index("region"), lax.axis_index("chan")
    mz, my, mx = r // 16, (r // 4) % 4, r % 4
    other = 1 - c

    def at_offset(g):
        return ((mz + g // 16) % 4) * 16 + ((my + (g // 4) % 4) % 4) * 4 + (mx + g % 4) % 4

    def remote(src, dst, send, recv, device):
        return pltpu.make_async_remote_copy(
            src_ref=src, dst_ref=dst, send_sem=send, recv_sem=recv,
            device_id=device, device_id_type=MESH,
        )

    def greet(device):
        pl.semaphore_signal(barrier, inc=1, device_id=device, device_id_type=MESH)

    barrier = pltpu.get_barrier_semaphore()
    for g in OFFSETS:
        greet((at_offset(g), c))
    greet((r, other))
    greet(((r + 63 + 2 * c) % 64, other))

    eye = iota((64, 64), 0) == iota((64, 64), 1)
    lower = (iota((64, 64), 1) < iota((64, 64), 0)).astype(F32).astype(BF16)
    hits, counts, starts = [], [], []
    before = jnp.zeros((1, 64), F32)
    for t in range(2):
        target = region_ref[:, t : t + 1]
        gz, gy, gx = (target // 16 - mz) & 3, ((target // 4) % 4 - my) & 3, (target % 4 - mx) & 3
        offset = gz * 16 + gy * 4 + gx
        hit = jnp.where(iota((64, 64), 1) == offset, 1.0, 0.0)
        count = jnp.dot(lower, hit.astype(BF16), preferred_element_type=F32) + before
        before = before + jnp.sum(hit, axis=0, keepdims=True)
        rank = jnp.sum(hit * count, axis=1, keepdims=True)
        hits.append(hit)
        counts.append(count)
        starts.append(offset.astype(F32) * 16.0 + rank)
    lane256 = iota((64, 256), 1)
    spread = iota((64, 256), 0) == lane256 % 64
    quarter = (4 * (iota((1, 256), 1) // 64)).astype(F32)
    rows_of = [
        jnp.sum(jnp.where(spread, s, 0.0), axis=0, keepdims=True) + quarter for s in starts
    ]
    stacked = jnp.concatenate([patches_ref[:, 1024 * q : 1024 * q + 1024] for q in range(4)], axis=0)
    for k in range(4):
        row = (iota((256, 256), 0) + 256 * k).astype(F32)
        chosen = jnp.where((row == rows_of[0]) | (row == rows_of[1]), 1.0, 0.0).astype(BF16)
        payload[16 * k : 16 * k + 16] = (
            jnp.dot(chosen, stacked, preferred_element_type=F32).astype(BF16).reshape(16, 16, 1024)
        )
    lane = iota((64, W), 1)
    codes = jnp.full((64, W), -1.0, F32)
    for k in range(4):
        value = jnp.zeros((1, 64), F32)
        for t in range(2):
            cell = cell_ref[:, t : t + 1].astype(F32) + 1.0
            value = value + jnp.sum(
                jnp.where(counts[t] == float(k), hits[t] * cell, 0.0), axis=0, keepdims=True
            )
        column = jnp.sum(jnp.where(eye, value, 0.0), axis=1, keepdims=True) - 1.0
        code = jnp.where(column >= 0.0, column + (32 * ((lane // 4) % 4)).astype(F32), -1.0)
        codes = jnp.where(lane % 4 == k, code, codes)
    cells_out[:, 0, :] = codes

    pl.semaphore_wait(barrier, 65)
    for g in OFFSETS:
        remote(cells_out.at[g], cells_in.at[g], cell_send, cell_recv, (at_offset(g), c)).start()
    for g in OFFSETS:
        remote(payload.at[g], arrived.at[g], a2a_send, a2a_recv, (at_offset(g), c)).start()
    arrived[0] = payload[0]
    cells_in[0] = cells_out[0]

    first_rows = pl.ds(pl.multiple_of(64 * c, 64), 64)
    second_rows = pl.ds(pl.multiple_of(128 * c, 128), 128)
    wf[first_rows, :] = jnp.concatenate([wf_ref[k] for k in range(9)], axis=1)
    for k in range(9):
        wd[second_rows, 128 * k : 128 * k + 128] = wd_ref[k]
        wp[second_rows, 256 * k : 256 * k + 256] = wp_ref[k]
    weight_copies = [
        remote(buf.at[rows], buf.at[rows], w_send.at[n], w_recv.at[n], (r, other))
        for n, (buf, rows) in enumerate([(wf, first_rows), (wd, second_rows), (wp, second_rows)])
    ]
    for copy in weight_copies:
        copy.start()
    for k in range(9):
        i, j = k // 3, k % 3
        wm[:, 1152 * i + 128 * j : 1152 * i + 128 * j + 128] = wm_ref[k, :, :C1]
        wm[:, 1152 * i + 384 + 256 * j : 1152 * i + 384 + 256 * j + 256] = wm_ref[k, :, C1:]
        wo[:, 128 * k : 128 * k + 128] = wo_ref[k]

    remote(
        cells_out.at[pl.ds(1, 63)], cells_in.at[pl.ds(1, 63)], cell_send, cell_recv, (r, other)
    ).wait_recv()
    owner = iota((8, W), 0) == iota((8, W), 1) // 16
    for b in range(8):
        code = jnp.sum(
            jnp.where(owner, cells_in[8 * b : 8 * b + 8, 0, :], 0.0), axis=0, keepdims=True
        )
        place[:, W * b : W * b + W] = jnp.where(
            iota((W, W), 0).astype(F32) == code, 1.0, 0.0
        ).astype(BF16)
    remote(
        payload.at[pl.ds(1, 63)], arrived.at[pl.ds(1, 63)], a2a_send, a2a_recv, (r, other)
    ).wait_recv()

    for n in range(4):
        sums = jnp.dot(
            place[...],
            arrived[:, :, 256 * n : 256 * n + 256].reshape(1024, 256),
            preferred_element_type=F32,
        )
        for h in range(2):
            block = swap_granules(sums[:, W * h : W * h + W])
            for q in range(4):
                for band in range(4):
                    at = 8 * (4 * q + band)
                    grid_f[pl.ds(256 * band + 8 * q + 2 * n + h, 8, stride=32), :] = block[at : at + 8]
    grid_own[...] = grid_f[...].astype(BF16).reshape(32, 32, W)

    own = pl.ds(pl.multiple_of(32 * c, 32), 32)
    grid_copies = [
        remote(
            grid_own.at[pl.ds(10 * other, 22)], grid.at[pl.ds(6 * c, 22), own],
            g_send.at[0], g_recv.at[2], (r, other),
        ),
        remote(
            grid_own.at[pl.ds(26, 6)], grid.at[pl.ds(0, 6), own],
            g_send.at[1], g_recv.at[c], ((r + 1) % 64, 0),
        ),
        remote(
            grid_own.at[pl.ds(0, 6)], grid.at[pl.ds(22, 6), own],
            g_send.at[2], g_recv.at[c], ((r + 63) % 64, 1),
        ),
    ]
    for copy in grid_copies:
        copy.start()
    grid[pl.ds(6 * other, 22), own, :] = grid_own[pl.ds(10 * c, 22)]
    grid_copies[0].wait_recv()
    for n in range(2):
        remote(
            grid_own.at[pl.ds(0, 6)], grid.at[pl.ds(0, 6), pl.ds(0, 32)],
            g_send.at[1], g_recv.at[n], (r, other),
        ).wait_recv()
    top = jnp.logical_and(r == 0, c == 0)
    bottom = jnp.logical_and(r == 63, c == 1)

    @pl.when(top)
    def _():
        grid[0:6] = jnp.zeros((6, C0, W), BF16)

    @pl.when(bottom)
    def _():
        grid[22:28] = jnp.zeros((6, C0, W), BF16)

    keep_top = jnp.where(top, 0.0, 1.0)
    keep_bottom = jnp.where(bottom, 0.0, 1.0)
    even = iota((C2, W), 1) % 2 == 0

    def cols(x):
        return jnp.concatenate([shift(x, -1), x, shift(x, 1)], axis=0)

    def widen(l, _):
        im1[l] = cols(grid[l].astype(F32)).astype(BF16)
        return 0

    lax.fori_loop(0, 28, widen, 0, unroll=4)
    for copy in weight_copies:
        copy.wait_recv()

    def first_rows_of(n, _):
        f = 4 * n
        window = jnp.concatenate(
            [im1[pl.ds(f + t, 3)].reshape(576, W) for t in range(4)], axis=1
        )
        total = jnp.dot(wf[...], window, preferred_element_type=F32)
        for t in range(4):
            factor = jnp.where(f + t < 5, keep_top, jnp.where(f + t >= 21, keep_bottom, 1.0))
            row = silu(total[:, W * t : W * t + W]) * factor
            im2[f + t, 0:384] = cols(row).astype(BF16)
        return 0

    lax.fori_loop(0, 7, first_rows_of, 0)

    def spread_pair(x):
        return jnp.concatenate([shift(x, -2), x, shift(x, 2)], axis=0).astype(BF16)

    pairs = []
    for m in range(6):
        window = jnp.concatenate(
            [
                jnp.concatenate([im2[4 * m + 2 * t + i, 0:384] for i in range(3)], axis=0)
                for t in range(2)
            ],
            axis=1,
        )
        total = jnp.dot(wd[...], window, preferred_element_type=F32)
        pair = silu(jnp.where(even, total[:, :W], pltpu.roll(total[:, W:], 1, 1)))
        if m == 0:
            pair = pair * keep_top
        if m == 5:
            pair = pair * keep_bottom
        pair = pair.astype(BF16).astype(F32)
        imd[2 * m] = spread_pair(pair)
    for m in range(5):
        a = imd[2 * m, C2 : 2 * C2].astype(F32)
        b = imd[2 * m + 2, C2 : 2 * C2].astype(F32)
        imd[2 * m + 1] = spread_pair(jnp.where(even, shift(a, 1), shift(b, -1)))

    for ms in ((0, 1), (2, 3), (4,)):
        window = jnp.concatenate([imd[2 * m : 2 * m + 3].reshape(2304, W) for m in ms], axis=1)
        total = jnp.dot(wp[...], window, preferred_element_type=F32)
        for t, m in enumerate(ms):
            third = silu(total[:, W * t : W * t + W]) + imd[2 * m + 1, C2 : 2 * C2].astype(F32)
            if m == 0:
                third = jnp.where(even, third * keep_top, third)
            if m == 4:
                third = jnp.where(even, third, third * keep_bottom)
            l1, l2, r1, r2 = shift(third, -1), shift(third, -2), shift(third, 1), shift(third, 2)
            edge = iota((C2, W), 1) < W - 1
            ups = (
                (
                    jnp.where(even, l2, l1),
                    jnp.where(even, third, l1),
                    jnp.where(edge, jnp.where(even, third, r1), 0.0),
                ),
                (
                    jnp.where(even, l1, third),
                    jnp.where(even, r1, third),
                    jnp.where(even, r1, r2),
                ),
            )
            for half in range(2):
                for j in range(3):
                    value = ups[half][j].astype(BF16)
                    if half == 0 and j == 0:
                        value = jnp.where(iota((C2, W), 1) == 0, 0.0, ups[half][j]).astype(BF16)
                    f = 4 * m + 3 + 2 * half
                    im2[f, 384 + C2 * j : 384 + C2 * j + C2] = value
                    im2[f + 1, 384 + C2 * j : 384 + C2 * j + C2] = value

    def fourth_rows(n, _):
        g = 2 * n
        window = jnp.concatenate(
            [im2[pl.ds(g + 3 + t, 3)].reshape(3456, W) for t in range(2)], axis=1
        )
        total = jnp.dot(wm[...], window, preferred_element_type=F32)
        for t in range(2):
            factor = jnp.where(g + t < 1, keep_top, jnp.where(g + t >= 17, keep_bottom, 1.0))
            im4[g + t] = cols(silu(total[:, W * t : W * t + W]) * factor).astype(BF16)
        return 0

    lax.fori_loop(0, 9, fourth_rows, 0)

    def out_rows(n, _):
        f = 4 * n
        window = jnp.concatenate(
            [im4[pl.ds(f + t, 3)].reshape(1152, W) for t in range(4)], axis=1
        )
        total = jnp.dot(wo[...], window, preferred_element_type=F32)
        for t in range(4):
            row = total[:, W * t : W * t + W] + grid[f + t + 6].astype(F32)
            out_f[pl.ds(f + t, C0, stride=HALF), :] = row
        return 0

    lax.fori_loop(0, 4, out_rows, 0)
    out_b[...] = out_f[...].astype(BF16).reshape(C0, HALF, W)
    mine = pl.ds(pl.multiple_of(HALF * c, HALF), HALF)
    out_copy = remote(
        out_b.at[pl.ds(32 * other, 32)], out_ref.at[:, mine, :], o_send, o_recv, (r, other)
    )
    out_copy.start()
    out_ref[:, mine, :] = out_b[pl.ds(32 * c, 32)]

    for copy in weight_copies + grid_copies:
        copy.wait_send()
    remote(
        cells_out.at[pl.ds(1, 63)], cells_in.at[pl.ds(1, 63)], cell_send, cell_recv, (r, other)
    ).wait_send()
    remote(
        payload.at[pl.ds(1, 63)], arrived.at[pl.ds(1, 63)], a2a_send, a2a_recv, (r, other)
    ).wait_send()
    out_copy.wait()


def shards(*args):
    vmem = pl.BlockSpec(memory_space=pltpu.VMEM)
    dma = pltpu.SemaphoreType.DMA
    return pl.pallas_call(
        kernel,
        out_shape=jax.ShapeDtypeStruct((32, 32, W), BF16),
        in_specs=[vmem] * 8,
        out_specs=vmem,
        scratch_shapes=[
            pltpu.VMEM((64, 16, 1024), BF16),
            pltpu.VMEM((64, 16, 1024), BF16),
            pltpu.VMEM((64, 1, W), F32),
            pltpu.VMEM((64, 1, W), F32),
            pltpu.VMEM((C1, 9 * C0), BF16),
            pltpu.VMEM((C2, 9 * C1), BF16),
            pltpu.VMEM((C2, 9 * C2), BF16),
            pltpu.VMEM((C1, 9 * (C1 + C2)), BF16),
            pltpu.VMEM((C0, 9 * C1), BF16),
            pltpu.VMEM((W, 1024), BF16),
            pltpu.VMEM((1024, W), F32),
            pltpu.VMEM((32, 32, W), BF16),
            pltpu.VMEM((28, C0, W), BF16),
            pltpu.VMEM((30, 3 * C0, W), BF16),
            pltpu.VMEM((28, 3 * (C1 + C2), W), BF16),
            pltpu.VMEM((11, 3 * C2, W), BF16),
            pltpu.VMEM((18, 3 * C1, W), BF16),
            pltpu.VMEM((C0 * HALF, W), F32),
            pltpu.VMEM((C0, HALF, W), BF16),
            dma, dma, dma, dma, dma((3,)), dma((3,)), dma((3,)), dma((3,)), dma, dma,
        ],
        compiler_params=pltpu.CompilerParams(
            collective_id=0, has_side_effects=True, vmem_limit_bytes=56 << 20
        ),
    )(*args)


def solution(mesh):
    placed = (
        P("region", "chan"),
        P("region", None),
        P("region", None),
        P(None, "chan", None),
        P(None, "chan", None),
        P(None, "chan", None),
        P(),
        P(),
    )
    return jax.shard_map(
        shards, mesh=mesh, in_specs=placed, out_specs=P("chan", "region", None), check_vma=False
    )
```

time: 287 us -> 63.4 us (0.22); the launches traced: 282 us -> 63.2 us
  waiting for transfers between devices: 93.3 us -> 0 us
  local copies, waits for them, and re-layouts: 86.4 us -> 3.77 us
  Pallas kernels: 0 us -> 59.4 us
  starting transfers between devices: 41.8 us -> 0 us
  matrix products: 29.6 us -> 0 us
  between operations: 14.1 us -> 0.01 us
  blocking collectives: 9.52 us -> 0 us
  other arithmetic: 7.53 us -> 0 us
    pallas_call x0 -> x1, Pallas kernels: none -> 59.4 us  [shards(): pl.pallas_call(kernel, out_shape=jax.ShapeDtypeStruct((32, 32, W), BF16),...]
    slice x19 -> x0, local copies, waits for them, and re-layouts: 44.3 us -> none  [the longest x11 43.8 us: conv_taps(): lax.slice(padded, (0, row_off, col_off), (chans, row_off + stride * (out_...]
    all_gather x2 -> x0, waiting for transfers between devices: 38.8 us -> none  [the longest x1 20 us: encode(): lax.all_gather(haloed, 'chan', axis=0, tiled=True)]
    dot_general x47 -> x0, matrix products: 29.6 us -> none  [the longest x36 22 us: conv_taps(): jnp.dot(weights[3 * row_off + col_off], window.reshape(chans, out_rows *...]
    all_to_all x2 -> x0, waiting for transfers between devices: 27.6 us -> none  [the longest x1 26.7 us: shards(): lax.all_to_all(payload, 'region', split_axis=0, concat_axis=0, tiled=True)]
    all_to_all x2 -> x0, starting transfers between devices: 20.9 us -> none  [the longest x1 12 us: shards(): lax.all_to_all(slot_cells, 'region', split_axis=0, concat_axis=0, tiled=T...]
    ppermute x10 -> x0, starting transfers between devices: 20.6 us -> none  [the longest x4 11 us: extended(): lax.ppermute(tail, axis, [(i, (i + 1) % count) for i in range(ends)])]
    ppermute x10 -> x0, waiting for transfers between devices: 14.5 us -> none  [the longest x4 11.1 us: extended(): lax.ppermute(head, axis, [((i + 1) % count, i) for i in range(ends)])]
  transfers between devices with their start and end apart: 15 -> 0, of which waited for: 10 -> 0; matrix products, arithmetic and copies ran while one was open for 6% -> 0% of each run, Pallas kernels for 0% -> 0%
where the time goes in v1:
time: 63.4 us; the launch traced here: 63.2 us
  Pallas kernels  59.4 us (94%)
  local copies, waits for them, and re-layouts  3.77 us (6%)
    pallas_call x1, Pallas kernels, shards(): pl.pallas_call(kernel, out_shape=jax.ShapeDtypeStruct((32, 32, W), BF16),...  59.4 us
    unnamed x5, local copies, waits for them, and re-layouts  3.77 us

profile of v1, /device:TPU:1, one launch (start us, length us, event | category | flops | bytes accessed | tf_op | source)
XLA Modules:
  0.0 63.2 jit_solution(8543325090680640016)
XLA Ops:
  0.0 0.0 copy-start
  0.0 1.4 %copy.9.region_ref = s32[64,2]{1,0:T(8,128)} copy(s32[64,2]{0,1:T(2,128)} %param.9) | data formatting | bytes 1024 | tf_op args[1]
  1.4 0.0 copy-done
  1.4 0.7 %copy.10.cell_ref = s32[64,2]{1,0:T(8,128)} copy(s32[64,2]{0,1:T(2,128)S(1)} %copy-done) | data formatting | bytes 1024 | tf_op args[2]
  2.1 59.4 %shard_map.82 = bf16[32,32,128]{2,1,0:T(8,128)(2,1)} custom-call(bf16[64,4096]{1,0:T(8,128)(2,1)} %patches_ref.1, s32[64,2]{1,0:T(8,128)} %copy.9.region_ref, s32[64,2]{1,0:T(8,128)} %copy.10.cell_ref, bf16[9,64,64]{2,1,0:T(8,128)(2,1)} %wf_ref.1, bf16[9,128,128]{2,1,0:T(8,128)(2,1)} %wd_ref.1, bf16[9,128,256]{2,1,0:T(8,128)(2,1)} %wp_ref.1, ...), custom_call_target="tpu_custom_call" | custom-call | tf_op jit(solution)/shard_map/pallas_call | solution.py:344
  61.5 1.7 %copy.12 = bf16[32,32,128]{2,1,0:T(8,128)(2,1)} copy(bf16[32,32,128]{2,1,0:T(8,128)(2,1)} %shard_map.82) | data formatting | bytes 524288
Async XLA Ops:
  0.0 1.4 %copy-start = (s32[64,2]{0,1:T(2,128)S(1)}, s32[64,2]{0,1:T(2,128)}, u32[]{:S(2)}) copy-start(s32[64,2]{0,1:T(2,128)} %param.10) | copy-start | bytes 1540

commit v2 on v1

v2 whole, which is shorter than its diff:
```python
import jax
import jax.numpy as jnp
from jax import lax
from jax.experimental import pallas as pl
from jax.experimental.pallas import tpu as pltpu
from jax.sharding import PartitionSpec as P

C0 = 64
C1 = 128
C2 = 256
W = 128
HALF = 16
F32 = jnp.float32
BF16 = jnp.bfloat16
MESH = pl.DeviceIdType.MESH

PARTS = (((0, 1, 2), (6, 5)), ((1, 2, 0), (6, 5)), ((2, 0, 1), (5, 5)))
STEPS = (2, 1, 3)


def jobs():
    chunks, start = [[], []], 0
    for p, (_, sizes) in enumerate(PARTS):
        for h, size in enumerate(sizes):
            chunks[h].append((p, W * start, W * (start + size)))
            start += size
    return chunks


def iota(shape, axis):
    return lax.broadcasted_iota(jnp.int32, shape, axis)


def shift(x, step):
    lane = iota(x.shape, 1)
    keep = lane < W - step if step > 0 else lane >= -step
    return jnp.where(keep, pltpu.roll(x, (-step) % W, 1), 0.0)


def silu(v):
    h = 0.5 * v
    return h + h * jnp.tanh(h)


def swap_granules(x):
    rows = x.shape[0]
    row, gran = iota(x.shape, 0), iota(x.shape, 1) // 16
    for s in (1, 2, 4):
        down = pltpu.roll(pltpu.roll(x, 16 * s, 1), rows - s, 0)
        up = pltpu.roll(pltpu.roll(x, W - 16 * s, 1), s, 0)
        row_bit, gran_bit = (row & s) != 0, (gran & s) != 0
        x = jnp.where(row_bit == gran_bit, x, jnp.where(gran_bit, down, up))
    return x


def kernel(
    patches_ref, region_ref, cell_ref, wf_ref, wd_ref, wp_ref, wm_ref, wo_ref,
    out_ref,
    gathered, slots_out, slots_in, sums_out, sums_in, sums_own, tables_out, tables_in, codes_out, codes_in,
    wf_raw, wd_raw, wp_raw, wm_raw, wo_raw,
    wf, wd, wp, wm, wo,
    select, place, grid_f, grid_own, grid, im1, im2, imd, im4, out_f, out_b,
    load, t_send, t_recv, c_send, c_recv, route_send, route_recv,
    w_send, w_recv, g_send, g_recv, o_send, o_recv,
):
    r, c = lax.axis_index("region"), lax.axis_index("chan")
    at = (r // 16, (r // 4) % 4, r % 4)
    other = 1 - c

    def along(axis, step):
        z, y, x = ((at[a] + step) % 4 if a == axis else at[a] for a in range(3))
        return (z * 16 + y * 4 + x, c)

    def remote(src, dst, send, recv, device):
        return pltpu.make_async_remote_copy(
            src_ref=src, dst_ref=dst, send_sem=send, recv_sem=recv,
            device_id=device, device_id_type=MESH,
        )

    def greet(device):
        pl.semaphore_signal(barrier, inc=1, device_id=device, device_id_type=MESH)

    barrier = pltpu.get_barrier_semaphore()
    for axis in range(3):
        for step in STEPS:
            greet(along(axis, step))
    greet((r, other))
    for core in range(2):
        greet(((r + 63 + 2 * c) % 64, core))

    loads = [
        pltpu.make_async_copy(src, dst, load.at[n])
        for n, (src, dst) in enumerate(
            [
                (patches_ref, gathered.at[0]), (wf_ref, wf_raw), (wd_ref, wd_raw),
                (wp_ref, wp_raw), (wm_ref, wm_raw), (wo_ref, wo_raw),
            ]
        )
    ]
    for copy in loads:
        copy.start()

    earlier = (iota((64, 64), 0) < iota((64, 64), 1)).astype(F32).astype(BF16)
    before = jnp.zeros((64, 1), F32)
    entry = jnp.zeros((8, 64), F32)
    for t in range(2):
        target = region_ref[t : t + 1, :]
        hit = jnp.where(iota((64, 64), 0) == target, 1.0, 0.0)
        count = jnp.dot(hit.astype(BF16), earlier, preferred_element_type=F32) + before
        before = before + jnp.sum(hit, axis=1, keepdims=True)
        rank = jnp.sum(hit * count, axis=0, keepdims=True)
        entry = jnp.where(iota((8, 64), 0) == t, target.astype(F32) * 4.0 + rank, entry)
        entry = jnp.where(
            iota((8, 64), 0) == t + 2, cell_ref[t : t + 1, :].astype(F32), entry
        )
    twice = (iota((64, W), 1) % 64 == iota((64, W), 0)).astype(F32).astype(BF16)
    tables_out[...] = jnp.dot(entry.astype(BF16), twice, preferred_element_type=F32)

    chunks = jobs()
    loads[0].wait()
    pl.semaphore_wait(barrier, 12)
    for axis in range(3):
        for step in STEPS:
            remote(
                tables_out, tables_in.at[axis, step], t_send, t_recv.at[axis], along(axis, step)
            ).start()
        tables_in[axis, 0] = tables_out[...]

    def spread_out(phase, h, src, dst):
        for step in STEPS:
            for p, a, b in chunks[h]:
                lanes = pl.ds(a, b - a)
                remote(
                    src(step).at[:, lanes], dst.at[step, :, lanes],
                    route_send.at[phase], route_recv.at[phase, h, p],
                    along(PARTS[p][0][phase], step),
                ).start()

    def arrive(phase, h, p, a, b, dst):
        whole = dst.at[pl.ds(1, 3), :, pl.ds(a, b - a)]
        remote(whole, whole, route_send.at[phase], route_recv.at[phase, h, p], (r, other)).wait_recv()

    for h in range(2):
        spread_out(0, h, lambda step: gathered.at[0], gathered)

    for copy in loads[1:]:
        copy.wait()
    first_rows = pl.ds(pl.multiple_of(64 * c, 64), 64)
    second_rows = pl.ds(pl.multiple_of(128 * c, 128), 128)
    wf[first_rows, :] = jnp.concatenate([wf_raw[k] for k in range(9)], axis=1)
    for k in range(9):
        wd[second_rows, 128 * k : 128 * k + 128] = wd_raw[k]
        wp[second_rows, 256 * k : 256 * k + 256] = wp_raw[k]
    weight_copies = [
        remote(buf.at[rows], buf.at[rows], w_send.at[n], w_recv.at[n], (r, other))
        for n, (buf, rows) in enumerate([(wf, first_rows), (wd, second_rows), (wp, second_rows)])
    ]
    for copy in weight_copies:
        copy.start()
    for k in range(9):
        i, j = k // 3, k % 3
        wm[:, 1152 * i + 128 * j : 1152 * i + 128 * j + 128] = wm_raw[k, :, :C1]
        wm[:, 1152 * i + 384 + 256 * j : 1152 * i + 384 + 256 * j + 256] = wm_raw[k, :, C1:]
        wo[:, 128 * k : 128 * k + 128] = wo_raw[k]

    lane = iota((8, W), 1)
    left = lane < 64
    for p, (axes, _) in enumerate(PARTS):
        here, second, third = axes
        three = tables_in.at[here, pl.ds(1, 3)]
        remote(three, three, t_send, t_recv.at[here], (r, other)).wait_recv()
        values = jnp.zeros((8, 256), F32)
        for half in range(2):
            table = jnp.where(left, tables_in[here, 2 * half], tables_in[here, 2 * half + 1])
            code = table.astype(jnp.int32)
            region = code // 4
            place_of = (region // 16, (region // 4) % 4, region % 4)
            slot = (
                ((place_of[second] - at[second]) & 3) * 64
                + (2 * half + lane // 64) * 16
                + ((place_of[third] - at[third]) & 3) * 4
                + code % 4
            )
            slot = jnp.where(place_of[here] == at[here], slot, -1)
            hits = [iota((256, W), 0) == slot[t : t + 1] for t in range(2)]
            select[p, :, W * half : W * half + W] = (
                jnp.where(jnp.logical_or(hits[0], hits[1]), 1.0, 0.0).astype(BF16)
            )
            for t in range(2):
                cells = jnp.broadcast_to(table[t + 2 : t + 3] + 1.0, (8, W)).astype(BF16)
                values = values + lax.dot_general(
                    cells, jnp.where(hits[t], 1.0, 0.0).astype(BF16),
                    (((1,), (1,)), ((), ())), preferred_element_type=F32,
                )
        for step in range(4):
            value = values[:, W * (step // 2) : W * (step // 2) + W]
            turned = pltpu.roll(value, 64, 1)
            value = jnp.where(left, value, turned) if step % 2 == 0 else jnp.where(left, turned, value)
            value = jnp.where(value > 0.0, value - 1.0 + (32 * ((lane // 4) % 4)).astype(F32), -1.0)
            if step == 0:
                codes_in[p, 0] = value
            else:
                codes_out[p, step] = value
        for step in STEPS:
            remote(
                codes_out.at[p, step], codes_in.at[p, step], c_send, c_recv.at[p], along(second, step)
            ).start()

    for h in range(2):
        for p, a, b in chunks[h]:
            arrive(0, h, p, a, b, gathered)
            for n in range(a, b, 256):
                e = min(n + 256, b)
                slots = jnp.dot(
                    select[p], gathered[:, :, n:e].reshape(256, e - n), preferred_element_type=F32
                ).astype(BF16)
                slots_in[0, :, n:e] = slots[:64]
                slots_out[:, :, n:e] = slots[64:].reshape(3, 64, e - n)
        spread_out(1, h, lambda step: slots_out.at[step - 1], slots_in)

    for p in range(3):
        three = codes_in.at[p, pl.ds(1, 3)]
        remote(three, three, c_send, c_recv.at[p], (r, other)).wait_recv()
        for half in range(2):
            code = jnp.where(left, codes_in[p, 2 * half], codes_in[p, 2 * half + 1])[0:1]
            place[p, :, W * half : W * half + W] = jnp.where(
                iota((W, W), 0).astype(F32) == code, 1.0, 0.0
            ).astype(BF16)
    for h in range(2):
        for p, a, b in chunks[h]:
            arrive(1, h, p, a, b, slots_in)
            for n in range(a, b, 256):
                e = min(n + 256, b)
                sums = jnp.dot(
                    place[p], slots_in[:, :, n:e].reshape(256, e - n), preferred_element_type=F32
                )
                sums_own[:, n:e] = sums[:32]
                sums_out[:, :, n:e] = sums[32:].astype(BF16).reshape(3, 32, e - n)
        spread_out(2, h, lambda step: sums_out.at[step - 1], sums_in)

    for h in range(2):
        for p, a, b in chunks[h]:
            arrive(2, h, p, a, b, sums_in)
            total = sums_own[:, a:b]
            for step in STEPS:
                total = total + sums_in[step, :, a:b].astype(F32)
            for n in range(a, b, W):
                block = swap_granules(total[:, n - a : n - a + W])
                for band in range(4):
                    grid_f[pl.ds(256 * band + n // W, 8, stride=32), :] = block[8 * band : 8 * band + 8]
    grid_own[...] = grid_f[...].astype(BF16).reshape(32, 32, W)

    own = pl.ds(pl.multiple_of(32 * c, 32), 32)
    grid_copies = [
        remote(
            grid_own.at[pl.ds(10 * other, 22)], grid.at[pl.ds(6 * c, 22), own],
            g_send.at[0], g_recv.at[2], (r, other),
        ),
        remote(
            grid_own.at[pl.ds(26, 6)], grid.at[pl.ds(0, 6), own],
            g_send.at[1], g_recv.at[c], ((r + 1) % 64, 0),
        ),
        remote(
            grid_own.at[pl.ds(0, 6)], grid.at[pl.ds(22, 6), own],
            g_send.at[2], g_recv.at[c], ((r + 63) % 64, 1),
        ),
    ]
    for copy in grid_copies:
        copy.start()
    grid[pl.ds(6 * other, 22), own, :] = grid_own[pl.ds(10 * c, 22)]
    grid_copies[0].wait_recv()
    top = jnp.logical_and(r == 0, c == 0)
    bottom = jnp.logical_and(r == 63, c == 1)
    keep_top = jnp.where(top, 0.0, 1.0)
    keep_bottom = jnp.where(bottom, 0.0, 1.0)
    even = iota((C2, W), 1) % 2 == 0

    def cols(x):
        return jnp.concatenate([shift(x, -1), x, shift(x, 1)], axis=0)

    def widen(l):
        im1[l] = cols(grid[l].astype(F32)).astype(BF16)

    def first_rows_of(k, _):
        f = 4 * ((k + 2 * other) % 7)
        window = jnp.concatenate(
            [im1[pl.ds(f + t, 3)].reshape(576, W) for t in range(4)], axis=1
        )
        total = jnp.dot(wf[...], window, preferred_element_type=F32)
        for t in range(4):
            factor = jnp.where(f + t < 5, keep_top, jnp.where(f + t >= 21, keep_bottom, 1.0))
            row = silu(total[:, W * t : W * t + W]) * factor
            im2[f + t, 0:384] = cols(row).astype(BF16)
        return 0

    def widen_own(l, _):
        widen(6 * other + l)
        return 0

    lax.fori_loop(0, 22, widen_own, 0, unroll=2)
    for copy in weight_copies:
        copy.wait_recv()
    lax.fori_loop(0, 5, first_rows_of, 0)
    for n in range(2):
        remote(
            grid_own.at[pl.ds(0, 6)], grid.at[pl.ds(0, 6), pl.ds(0, 32)],
            g_send.at[1], g_recv.at[n], (r, other),
        ).wait_recv()

    @pl.when(top)
    def _():
        grid[0:6] = jnp.zeros((6, C0, W), BF16)

    @pl.when(bottom)
    def _():
        grid[22:28] = jnp.zeros((6, C0, W), BF16)

    for l in range(6):
        widen(22 * c + l)
    lax.fori_loop(5, 7, first_rows_of, 0)

    def spread_pair(x):
        return jnp.concatenate([shift(x, -2), x, shift(x, 2)], axis=0).astype(BF16)

    pairs = []
    for m in range(6):
        window = jnp.concatenate(
            [
                jnp.concatenate([im2[4 * m + 2 * t + i, 0:384] for i in range(3)], axis=0)
                for t in range(2)
            ],
            axis=1,
        )
        total = jnp.dot(wd[...], window, preferred_element_type=F32)
        pair = silu(jnp.where(even, total[:, :W], pltpu.roll(total[:, W:], 1, 1)))
        if m == 0:
            pair = pair * keep_top
        if m == 5:
            pair = pair * keep_bottom
        pair = pair.astype(BF16).astype(F32)
        imd[2 * m] = spread_pair(pair)
    for m in range(5):
        a = imd[2 * m, C2 : 2 * C2].astype(F32)
        b = imd[2 * m + 2, C2 : 2 * C2].astype(F32)
        imd[2 * m + 1] = spread_pair(jnp.where(even, shift(a, 1), shift(b, -1)))

    for ms in ((0, 1), (2, 3), (4,)):
        window = jnp.concatenate([imd[2 * m : 2 * m + 3].reshape(2304, W) for m in ms], axis=1)
        total = jnp.dot(wp[...], window, preferred_element_type=F32)
        for t, m in enumerate(ms):
            third = silu(total[:, W * t : W * t + W]) + imd[2 * m + 1, C2 : 2 * C2].astype(F32)
            if m == 0:
                third = jnp.where(even, third * keep_top, third)
            if m == 4:
                third = jnp.where(even, third, third * keep_bottom)
            l1, l2, r1, r2 = shift(third, -1), shift(third, -2), shift(third, 1), shift(third, 2)
            edge = iota((C2, W), 1) < W - 1
            ups = (
                (
                    jnp.where(even, l2, l1),
                    jnp.where(even, third, l1),
                    jnp.where(edge, jnp.where(even, third, r1), 0.0),
                ),
                (
                    jnp.where(even, l1, third),
                    jnp.where(even, r1, third),
                    jnp.where(even, r1, r2),
                ),
            )
            for half in range(2):
                for j in range(3):
                    value = ups[half][j].astype(BF16)
                    if half == 0 and j == 0:
                        value = jnp.where(iota((C2, W), 1) == 0, 0.0, ups[half][j]).astype(BF16)
                    f = 4 * m + 3 + 2 * half
                    im2[f, 384 + C2 * j : 384 + C2 * j + C2] = value
                    im2[f + 1, 384 + C2 * j : 384 + C2 * j + C2] = value

    def fourth_rows(n, _):
        g = 2 * n
        window = jnp.concatenate(
            [im2[pl.ds(g + 3 + t, 3)].reshape(3456, W) for t in range(2)], axis=1
        )
        total = jnp.dot(wm[...], window, preferred_element_type=F32)
        for t in range(2):
            factor = jnp.where(g + t < 1, keep_top, jnp.where(g + t >= 17, keep_bottom, 1.0))
            im4[g + t] = cols(silu(total[:, W * t : W * t + W]) * factor).astype(BF16)
        return 0

    lax.fori_loop(0, 9, fourth_rows, 0)

    def out_rows(n, _):
        f = 4 * n
        window = jnp.concatenate(
            [im4[pl.ds(f + t, 3)].reshape(1152, W) for t in range(4)], axis=1
        )
        total = jnp.dot(wo[...], window, preferred_element_type=F32)
        for t in range(4):
            row = total[:, W * t : W * t + W] + grid[f + t + 6].astype(F32)
            out_f[pl.ds(f + t, C0, stride=HALF), :] = row
        return 0

    lax.fori_loop(0, 4, out_rows, 0)
    out_b[...] = out_f[...].astype(BF16).reshape(C0, HALF, W)
    mine = pl.ds(pl.multiple_of(HALF * c, HALF), HALF)
    out_copy = remote(
        out_b.at[pl.ds(32 * other, 32)], out_ref.at[:, mine, :], o_send, o_recv, (r, other)
    )
    out_copy.start()
    out_ref[:, mine, :] = out_b[pl.ds(32 * c, 32)]

    for copy in weight_copies + grid_copies:
        copy.wait_send()
    for phase, buffer in enumerate((gathered, slots_in, sums_in)):
        whole = buffer.at[pl.ds(1, 3)]
        remote(whole, whole, route_send.at[phase], o_recv, (r, other)).wait_send()
    three = tables_in.at[:, pl.ds(1, 3)]
    remote(three, three, t_send, o_recv, (r, other)).wait_send()
    three = codes_in.at[:, pl.ds(1, 3)]
    remote(three, three, c_send, o_recv, (r, other)).wait_send()
    out_copy.wait()


def shards(patches, region, cell, *weights):
    vmem = pl.BlockSpec(memory_space=pltpu.VMEM)
    anywhere = pl.BlockSpec(memory_space=pl.ANY)
    dma = pltpu.SemaphoreType.DMA
    return pl.pallas_call(
        kernel,
        out_shape=jax.ShapeDtypeStruct((32, 32, W), BF16),
        in_specs=[anywhere, vmem, vmem] + [anywhere] * 5,
        out_specs=vmem,
        scratch_shapes=[
            pltpu.VMEM((4, 64, 4096), BF16),
            pltpu.VMEM((3, 64, 4096), BF16),
            pltpu.VMEM((4, 64, 4096), BF16),
            pltpu.VMEM((3, 32, 4096), BF16),
            pltpu.VMEM((4, 32, 4096), BF16),
            pltpu.VMEM((32, 4096), F32),
            pltpu.VMEM((8, W), F32),
            pltpu.VMEM((3, 4, 8, W), F32),
            pltpu.VMEM((3, 4, 8, W), F32),
            pltpu.VMEM((3, 4, 8, W), F32),
            pltpu.VMEM((9, 64, C0), BF16),
            pltpu.VMEM((9, 128, C1), BF16),
            pltpu.VMEM((9, 128, C2), BF16),
            pltpu.VMEM((9, C1, C1 + C2), BF16),
            pltpu.VMEM((9, C0, C1), BF16),
            pltpu.VMEM((C1, 9 * C0), BF16),
            pltpu.VMEM((C2, 9 * C1), BF16),
            pltpu.VMEM((C2, 9 * C2), BF16),
            pltpu.VMEM((C1, 9 * (C1 + C2)), BF16),
            pltpu.VMEM((C0, 9 * C1), BF16),
            pltpu.VMEM((3, 256, 256), BF16),
            pltpu.VMEM((3, W, 256), BF16),
            pltpu.VMEM((1024, W), F32),
            pltpu.VMEM((32, 32, W), BF16),
            pltpu.VMEM((28, C0, W), BF16),
            pltpu.VMEM((30, 3 * C0, W), BF16),
            pltpu.VMEM((28, 3 * (C1 + C2), W), BF16),
            pltpu.VMEM((11, 3 * C2, W), BF16),
            pltpu.VMEM((18, 3 * C1, W), BF16),
            pltpu.VMEM((C0 * HALF, W), F32),
            pltpu.VMEM((C0, HALF, W), BF16),
            dma((6,)), dma, dma((3,)), dma, dma((3,)), dma((3,)), dma((3, 2, 3)),
            dma((3,)), dma((3,)), dma((3,)), dma((3,)), dma, dma,
        ],
        compiler_params=pltpu.CompilerParams(
            collective_id=0, has_side_effects=True, vmem_limit_bytes=56 << 20
        ),
    )(patches, region.T, cell.T, *weights)


def solution(mesh):
    placed = (
        P("region", "chan"),
        P("region", None),
        P("region", None),
        P(None, "chan", None),
        P(None, "chan", None),
        P(None, "chan", None),
        P(),
        P(),
    )
    return jax.shard_map(
        shards, mesh=mesh, in_specs=placed, out_specs=P("chan", "region", None), check_vma=False
    )
```

time: 63.4 us -> 52.2 us (0.82)
  Pallas kernels: 59.4 us -> 50.4 us
  local copies, waits for them, and re-layouts: 3.77 us -> 1.67 us
    pallas_call x1, Pallas kernels: 59.4 us -> 50.4 us  [shards(): pl.pallas_call(kernel, out_shape=jax.ShapeDtypeStruct((32, 32, W), BF16),...]
    unnamed x5 -> x1, local copies, waits for them, and re-layouts: 3.77 us -> 1.67 us
where the time goes in v2:
time: 52.2 us; the launch traced here: 52 us
  Pallas kernels  50.4 us (97%)
  local copies, waits for them, and re-layouts  1.67 us (3%)
    pallas_call x1, Pallas kernels, shards(): pl.pallas_call(kernel, out_shape=jax.ShapeDtypeStruct((32, 32, W), BF16),...  50.4 us
    unnamed x1, local copies, waits for them, and re-layouts  1.67 us

profile of v2, /device:TPU:1, one launch (start us, length us, event | category | flops | bytes accessed | tf_op | source)
XLA Modules:
  0.0 52.0 jit_solution(11076986641595802282)
XLA Ops:
  0.0 50.4 %shard_map.82 = bf16[32,32,128]{2,1,0:T(8,128)(2,1)} custom-call(bf16[64,4096]{1,0:T(8,128)(2,1)} %patches_ref.1, s32[2,64]{1,0:T(2,128)} %bitcast.2, s32[2,64]{1,0:T(2,128)} %bitcast.3, bf16[9,64,64]{2,1,0:T(8,128)(2,1)} %wf_ref.1, bf16[9,128,128]{2,1,0:T(8,128)(2,1)} %wd_ref.1, bf16[9,128,256]{2,1,0:T(8,128)(2,1)} %wp_ref.1, bf16[9,128,384]{2,1,0:T(8,128)(2,1)} %wm_ref.1, ...), custom_call_target="tpu_custom_call" | custom-call | tf_op jit(solution)/shard_map/pallas_call | solution.py:428
  50.4 1.7 %copy.10 = bf16[32,32,128]{2,1,0:T(8,128)(2,1)} copy(bf16[32,32,128]{2,1,0:T(8,128)(2,1)} %shard_map.82) | data formatting | bytes 524288

commit v3 on v2

--- a/solution.py
+++ b/solution.py
@@ -14,16 +14,17 @@
 BF16 = jnp.bfloat16
 MESH = pl.DeviceIdType.MESH
 
-PARTS = (((0, 1, 2), (6, 5)), ((1, 2, 0), (6, 5)), ((2, 0, 1), (5, 5)))
+PARTS = (((0, 1, 2), (6, 3, 2)), ((1, 2, 0), (5, 3, 3)), ((2, 0, 1), (5, 2, 3)))
 STEPS = (2, 1, 3)
 
 
 def jobs():
-    chunks, start = [[], []], 0
-    for p, (_, sizes) in enumerate(PARTS):
-        for h, size in enumerate(sizes):
-            chunks[h].append((p, W * start, W * (start + size)))
-            start += size
+    chunks, start = [], 0
+    for h in range(3):
+        chunks.append([])
+        for p, (_, sizes) in enumerate(PARTS):
+            chunks[h].append((p, W * start, W * (start + sizes[h])))
+            start += sizes[h]
     return chunks
 
 
@@ -34,7 +35,7 @@
 def shift(x, step):
     lane = iota(x.shape, 1)
     keep = lane < W - step if step > 0 else lane >= -step
-    return jnp.where(keep, pltpu.roll(x, (-step) % W, 1), 0.0)
+    return jnp.where(keep, pltpu.roll(x, (-step) % W, 1), jnp.zeros_like(x))
 
 
 def silu(v):
@@ -59,9 +60,9 @@
     gathered, slots_out, slots_in, sums_out, sums_in, sums_own, tables_out, tables_in, codes_out, codes_in,
     wf_raw, wd_raw, wp_raw, wm_raw, wo_raw,
     wf, wd, wp, wm, wo,
-    select, place, grid_f, grid_own, grid, im1, im2, imd, im4, out_f, out_b,
+    select, place, grid_f, tile, halo, im1, im2, imd, im4, out_f, out_b,
     load, t_send, t_recv, c_send, c_recv, route_send, route_recv,
-    w_send, w_recv, g_send, g_recv, o_send, o_recv,
+    w_send, w_recv, x_send, x_recv, h_send, h_recv, o_send, o_recv,
 ):
     r, c = lax.axis_index("region"), lax.axis_index("chan")
     at = (r // 16, (r // 4) % 4, r % 4)
@@ -85,8 +86,6 @@
         for step in STEPS:
             greet(along(axis, step))
     greet((r, other))
-    for core in range(2):
-        greet(((r + 63 + 2 * c) % 64, core))
 
     loads = [
         pltpu.make_async_copy(src, dst, load.at[n])
@@ -118,7 +117,7 @@
 
     chunks = jobs()
     loads[0].wait()
-    pl.semaphore_wait(barrier, 12)
+    pl.semaphore_wait(barrier, 10)
     for axis in range(3):
         for step in STEPS:
             remote(
@@ -140,7 +139,7 @@
         whole = dst.at[pl.ds(1, 3), :, pl.ds(a, b - a)]
         remote(whole, whole, route_send.at[phase], route_recv.at[phase, h, p], (r, other)).wait_recv()
 
-    for h in range(2):
+    for h in range(3):
         spread_out(0, h, lambda step: gathered.at[0], gathered)
 
     for copy in loads[1:]:
@@ -206,7 +205,7 @@
                 codes_out.at[p, step], codes_in.at[p, step], c_send, c_recv.at[p], along(second, step)
             ).start()
 
-    for h in range(2):
+    for h in range(3):
         for p, a, b in chunks[h]:
             arrive(0, h, p, a, b, gathered)
             for n in range(a, b, 256):
@@ -226,7 +225,7 @@
             place[p, :, W * half : W * half + W] = jnp.where(
                 iota((W, W), 0).astype(F32) == code, 1.0, 0.0
             ).astype(BF16)
-    for h in range(2):
+    for h in range(3):
         for p, a, b in chunks[h]:
             arrive(1, h, p, a, b, slots_in)
             for n in range(a, b, 256):
@@ -238,7 +237,37 @@
                 sums_out[:, :, n:e] = sums[32:].astype(BF16).reshape(3, 32, e - n)
         spread_out(2, h, lambda step: sums_out.at[step - 1], sums_in)
 
-    for h in range(2):
+    top = jnp.logical_and(r == 0, c == 0)
+    bottom = jnp.logical_and(r == 63, c == 1)
+    keep_top = jnp.where(top, 0.0, 1.0)
+    keep_bottom = jnp.where(bottom, 0.0, 1.0)
+    even = iota((C2, W), 1) % 2 == 0
+
+    def taps(x):
+        return shift(x, -1), x, shift(x, 1)
+
+    def settle(e):
+        mine = pl.ds(pl.multiple_of(32 * c + 16 * e, 16), 16)
+        tile[:, mine, :] = grid_f[e].astype(BF16).reshape(32, 16, W)
+        copy = remote(tile.at[:, mine], tile.at[:, mine], x_send.at[e], x_recv.at[e], (r, other))
+        copy.start()
+        return copy
+
+    own_rows = tile.at[pl.ds(10 * c, 22)]
+    own_im1 = im1.at[pl.ds(6 * other, 22)]
+
+    def widen(e, core):
+        source = own_rows.at[:, pl.ds(pl.multiple_of(32 * core + 16 * e, 16), 16)]
+        target = [
+            own_im1.at[:, pl.ds(pl.multiple_of(C0 * j + 32 * core + 16 * e, 16), 16)]
+            for j in range(3)
+        ]
+        for l in range(22):
+            for j, tap in enumerate(taps(source[l])):
+                target[j][l] = tap
+
+    tile_copies = []
+    for h in range(3):
         for p, a, b in chunks[h]:
             arrive(2, h, p, a, b, sums_in)
             total = sums_own[:, a:b]
@@ -246,162 +275,158 @@
                 total = total + sums_in[step, :, a:b].astype(F32)
             for n in range(a, b, W):
                 block = swap_granules(total[:, n - a : n - a + W])
+                e, ch = n // W // 16, n // W % 16
                 for band in range(4):
-                    grid_f[pl.ds(256 * band + n // W, 8, stride=32), :] = block[8 * band : 8 * band + 8]
-    grid_own[...] = grid_f[...].astype(BF16).reshape(32, 32, W)
-
-    own = pl.ds(pl.multiple_of(32 * c, 32), 32)
-    grid_copies = [
-        remote(
-            grid_own.at[pl.ds(10 * other, 22)], grid.at[pl.ds(6 * c, 22), own],
-            g_send.at[0], g_recv.at[2], (r, other),
-        ),
-        remote(
-            grid_own.at[pl.ds(26, 6)], grid.at[pl.ds(0, 6), own],
-            g_send.at[1], g_recv.at[c], ((r + 1) % 64, 0),
-        ),
-        remote(
-            grid_own.at[pl.ds(0, 6)], grid.at[pl.ds(22, 6), own],
-            g_send.at[2], g_recv.at[c], ((r + 63) % 64, 1),
-        ),
-    ]
-    for copy in grid_copies:
-        copy.start()
-    grid[pl.ds(6 * other, 22), own, :] = grid_own[pl.ds(10 * c, 22)]
-    grid_copies[0].wait_recv()
-    top = jnp.logical_and(r == 0, c == 0)
-    bottom = jnp.logical_and(r == 63, c == 1)
-    keep_top = jnp.where(top, 0.0, 1.0)
-    keep_bottom = jnp.where(bottom, 0.0, 1.0)
-    even = iota((C2, W), 1) % 2 == 0
-
-    def cols(x):
-        return jnp.concatenate([shift(x, -1), x, shift(x, 1)], axis=0)
-
-    def widen(l):
-        im1[l] = cols(grid[l].astype(F32)).astype(BF16)
-
-    def first_rows_of(k, _):
-        f = 4 * ((k + 2 * other) % 7)
+                    grid_f[e, pl.ds(W * band + ch, 8, stride=16), :] = block[8 * band : 8 * band + 8]
+        if h != 1:
+            e = h // 2
+            tile_copies.append(settle(e))
+            widen(e, c)
+            tile_copies[e].wait_recv()
+            if e == 1:
+                halo_copy = remote(
+                    tile.at[pl.ds(26 * other, 6)], halo, h_send, h_recv, ((r + 1 + 62 * c) % 64, c)
+                )
+                halo_copy.start()
+            widen(e, other)
+    for copy in weight_copies:
+        copy.wait_recv()
+
+    def first_rows_of(base, n, source, target):
+        f = 4 * n
         window = jnp.concatenate(
-            [im1[pl.ds(f + t, 3)].reshape(576, W) for t in range(4)], axis=1
+            [source[f + t : f + t + 3].reshape(576, W) for t in range(4)], axis=1
         )
         total = jnp.dot(wf[...], window, preferred_element_type=F32)
         for t in range(4):
-            factor = jnp.where(f + t < 5, keep_top, jnp.where(f + t >= 21, keep_bottom, 1.0))
-            row = silu(total[:, W * t : W * t + W]) * factor
-            im2[f + t, 0:384] = cols(row).astype(BF16)
-        return 0
-
-    def widen_own(l, _):
-        widen(6 * other + l)
-        return 0
-
-    lax.fori_loop(0, 22, widen_own, 0, unroll=2)
-    for copy in weight_copies:
-        copy.wait_recv()
-    lax.fori_loop(0, 5, first_rows_of, 0)
-    for n in range(2):
-        remote(
-            grid_own.at[pl.ds(0, 6)], grid.at[pl.ds(0, 6), pl.ds(0, 32)],
-            g_send.at[1], g_recv.at[n], (r, other),
-        ).wait_recv()
-
-    @pl.when(top)
-    def _():
-        grid[0:6] = jnp.zeros((6, C0, W), BF16)
-
-    @pl.when(bottom)
-    def _():
-        grid[22:28] = jnp.zeros((6, C0, W), BF16)
-
-    for l in range(6):
-        widen(22 * c + l)
-    lax.fori_loop(5, 7, first_rows_of, 0)
-
-    def spread_pair(x):
-        return jnp.concatenate([shift(x, -2), x, shift(x, 2)], axis=0).astype(BF16)
-
-    pairs = []
-    for m in range(6):
+            at_row = base + f + t
+            factor = jnp.where(at_row < 5, keep_top, jnp.where(at_row >= 21, keep_bottom, 1.0))
+            row = (silu(total[:, W * t : W * t + W]) * factor).astype(BF16)
+            for j, tap in enumerate(taps(row)):
+                target[f + t, C1 * j : C1 * j + C1] = tap
+
+    def spread_pair(target, at_pair, x):
+        for j, tap in enumerate((shift(x, -2), x, shift(x, 2))):
+            target[at_pair, C2 * j : C2 * j + C2] = tap
+
+    def second_pair(base, m, source, target):
         window = jnp.concatenate(
             [
-                jnp.concatenate([im2[4 * m + 2 * t + i, 0:384] for i in range(3)], axis=0)
+                jnp.concatenate([source[4 * m + 2 * t + i, 0:384] for i in range(3)], axis=0)
                 for t in range(2)
             ],
             axis=1,
         )
         total = jnp.dot(wd[...], window, preferred_element_type=F32)
         pair = silu(jnp.where(even, total[:, :W], pltpu.roll(total[:, W:], 1, 1)))
-        if m == 0:
-            pair = pair * keep_top
-        if m == 5:
-            pair = pair * keep_bottom
-        pair = pair.astype(BF16).astype(F32)
-        imd[2 * m] = spread_pair(pair)
-    for m in range(5):
-        a = imd[2 * m, C2 : 2 * C2].astype(F32)
-        b = imd[2 * m + 2, C2 : 2 * C2].astype(F32)
-        imd[2 * m + 1] = spread_pair(jnp.where(even, shift(a, 1), shift(b, -1)))
-
-    for ms in ((0, 1), (2, 3), (4,)):
-        window = jnp.concatenate([imd[2 * m : 2 * m + 3].reshape(2304, W) for m in ms], axis=1)
+        at_pair = base + m
+        factor = jnp.where(at_pair == 0, keep_top, jnp.where(at_pair == 5, keep_bottom, 1.0))
+        spread_pair(target, 2 * m, (pair * factor).astype(BF16))
+
+    def blend(m, target):
+        a, b = target[2 * m, C2 : 2 * C2], target[2 * m + 2, C2 : 2 * C2]
+        spread_pair(target, 2 * m + 1, jnp.where(even, shift(a, 1), shift(b, -1)))
+
+    def third_pairs(base, ms, source, target):
+        window = jnp.concatenate(
+            [source[2 * m : 2 * m + 3].reshape(2304, W) for m in ms], axis=1
+        )
         total = jnp.dot(wp[...], window, preferred_element_type=F32)
         for t, m in enumerate(ms):
-            third = silu(total[:, W * t : W * t + W]) + imd[2 * m + 1, C2 : 2 * C2].astype(F32)
-            if m == 0:
-                third = jnp.where(even, third * keep_top, third)
-            if m == 4:
-                third = jnp.where(even, third, third * keep_bottom)
+            third = silu(total[:, W * t : W * t + W]) + source[2 * m + 1, C2 : 2 * C2].astype(F32)
+            factor = jnp.where(
+                even,
+                jnp.where(base + m == 0, keep_top, 1.0),
+                jnp.where(base + m == 4, keep_bottom, 1.0),
+            )
+            third = (third * factor).astype(BF16)
             l1, l2, r1, r2 = shift(third, -1), shift(third, -2), shift(third, 1), shift(third, 2)
-            edge = iota((C2, W), 1) < W - 1
+            lane = iota((C2, W), 1)
             ups = (
                 (
                     jnp.where(even, l2, l1),
                     jnp.where(even, third, l1),
-                    jnp.where(edge, jnp.where(even, third, r1), 0.0),
+                    jnp.where(lane == W - 1, jnp.zeros_like(third), jnp.where(even, third, r1)),
                 ),
                 (
-                    jnp.where(even, l1, third),
+                    jnp.where(lane == 0, jnp.zeros_like(third), jnp.where(even, l1, third)),
                     jnp.where(even, r1, third),
                     jnp.where(even, r1, r2),
                 ),
             )
             for half in range(2):
                 for j in range(3):
-                    value = ups[half][j].astype(BF16)
-                    if half == 0 and j == 0:
-                        value = jnp.where(iota((C2, W), 1) == 0, 0.0, ups[half][j]).astype(BF16)
                     f = 4 * m + 3 + 2 * half
-                    im2[f, 384 + C2 * j : 384 + C2 * j + C2] = value
-                    im2[f + 1, 384 + C2 * j : 384 + C2 * j + C2] = value
-
-    def fourth_rows(n, _):
+                    target[f, 384 + C2 * j : 384 + C2 * j + C2] = ups[half][j]
+                    target[f + 1, 384 + C2 * j : 384 + C2 * j + C2] = ups[half][j]
+
+    def fourth_rows(base, n, source, target):
         g = 2 * n
         window = jnp.concatenate(
-            [im2[pl.ds(g + 3 + t, 3)].reshape(3456, W) for t in range(2)], axis=1
+            [source[g + 3 + t : g + 6 + t].reshape(3456, W) for t in range(2)], axis=1
         )
         total = jnp.dot(wm[...], window, preferred_element_type=F32)
         for t in range(2):
-            factor = jnp.where(g + t < 1, keep_top, jnp.where(g + t >= 17, keep_bottom, 1.0))
-            im4[g + t] = cols(silu(total[:, W * t : W * t + W]) * factor).astype(BF16)
-        return 0
-
-    lax.fori_loop(0, 9, fourth_rows, 0)
-
-    def out_rows(n, _):
+            at_row = base + g + t
+            factor = jnp.where(at_row < 1, keep_top, jnp.where(at_row >= 17, keep_bottom, 1.0))
+            row = (silu(total[:, W * t : W * t + W]) * factor).astype(BF16)
+            for j, tap in enumerate(taps(row)):
+                target[g + t, C1 * j : C1 * j + C1] = tap
+
+    def out_rows(n, source, skip, target):
         f = 4 * n
         window = jnp.concatenate(
-            [im4[pl.ds(f + t, 3)].reshape(1152, W) for t in range(4)], axis=1
+            [source[f + t : f + t + 3].reshape(1152, W) for t in range(4)], axis=1
         )
         total = jnp.dot(wo[...], window, preferred_element_type=F32)
         for t in range(4):
-            row = total[:, W * t : W * t + W] + grid[f + t + 6].astype(F32)
-            out_f[pl.ds(f + t, C0, stride=HALF), :] = row
-        return 0
-
-    lax.fori_loop(0, 4, out_rows, 0)
-    out_b[...] = out_f[...].astype(BF16).reshape(C0, HALF, W)
+            row = total[:, W * t : W * t + W] + skip[f + t].astype(F32)
+            target[pl.ds(f + t, C0, stride=8), :] = row
+
+    base = 8 * other
+    at_first, at_im2 = im1.at[pl.ds(base, 22)], im2.at[pl.ds(base, 20)]
+    at_imd, at_im4 = imd.at[pl.ds(4 * other, 7)], im4.at[pl.ds(base, 10)]
+    for n in range(5):
+        first_rows_of(base, n, at_first, at_im2)
+    for m in range(4):
+        second_pair(2 * other, m, at_im2, at_imd)
+    for m in range(3):
+        blend(m, at_imd)
+    third_pairs(2 * other, [0, 1], at_imd, at_im2)
+    third_pairs(2 * other, [2], at_imd, at_im2)
+    for n in range(5):
+        fourth_rows(base, n, at_im2, at_im4)
+    for n in range(2):
+        out_rows(n, at_im4, tile.at[pl.ds(8 + 8 * c, 8)], out_f.at[other])
+    halo_copy.wait_recv()
+
+    @pl.when(jnp.logical_or(top, bottom))
+    def _():
+        halo[...] = jnp.zeros((6, C0, W), BF16)
+
+    at_first, at_im2 = im1.at[pl.ds(22 * c, 6)], im2.at[pl.ds(20 * c, 8)]
+    for l in range(6):
+        for j, tap in enumerate(taps(halo[l])):
+            at_first[l, C0 * j : C0 * j + C0] = tap
+    at_first = im1.at[pl.ds(20 * c, 10)]
+    for n in range(2):
+        first_rows_of(20 * c, n, at_first, at_im2)
+    at_im2, at_imd = im2.at[pl.ds(16 * c, 9)], imd.at[pl.ds(8 * c, 3)]
+    for m in range(2):
+        second_pair(4 * c, m, at_im2, at_imd)
+    at_im2, at_imd = im2.at[pl.ds(12 * c, 11)], imd.at[pl.ds(6 * c, 5)]
+    for m in range(2):
+        blend(m, at_imd)
+    third_pairs(3 * c, [0, 1], at_imd, at_im2)
+    at_im2, at_im4 = im2.at[pl.ds(10 * c, 13)], im4.at[pl.ds(10 * c, 8)]
+    for n in range(4):
+        fourth_rows(10 * c, n, at_im2, at_im4)
+    at_im4 = im4.at[pl.ds(8 * c, 10)]
+    for n in range(2):
+        out_rows(n, at_im4, tile.at[pl.ds(24 * c, 8)], out_f.at[c])
+    out_b[...] = jnp.concatenate(
+        [out_f[n].reshape(C0, 8, W) for n in range(2)], axis=1
+    ).astype(BF16)
     mine = pl.ds(pl.multiple_of(HALF * c, HALF), HALF)
     out_copy = remote(
         out_b.at[pl.ds(32 * other, 32)], out_ref.at[:, mine, :], o_send, o_recv, (r, other)
@@ -409,7 +434,7 @@
     out_copy.start()
     out_ref[:, mine, :] = out_b[pl.ds(32 * c, 32)]
 
-    for copy in weight_copies + grid_copies:
+    for copy in weight_copies + tile_copies + [halo_copy]:
         copy.wait_send()
     for phase, buffer in enumerate((gathered, slots_in, sums_in)):
         whole = buffer.at[pl.ds(1, 3)]
@@ -453,17 +478,17 @@
             pltpu.VMEM((C0, 9 * C1), BF16),
             pltpu.VMEM((3, 256, 256), BF16),
             pltpu.VMEM((3, W, 256), BF16),
-            pltpu.VMEM((1024, W), F32),
-            pltpu.VMEM((32, 32, W), BF16),
-            pltpu.VMEM((28, C0, W), BF16),
+            pltpu.VMEM((2, 512, W), F32),
+            pltpu.VMEM((32, C0, W), BF16),
+            pltpu.VMEM((6, C0, W), BF16),
             pltpu.VMEM((30, 3 * C0, W), BF16),
             pltpu.VMEM((28, 3 * (C1 + C2), W), BF16),
             pltpu.VMEM((11, 3 * C2, W), BF16),
             pltpu.VMEM((18, 3 * C1, W), BF16),
-            pltpu.VMEM((C0 * HALF, W), F32),
+            pltpu.VMEM((2, C0 * 8, W), F32),
             pltpu.VMEM((C0, HALF, W), BF16),
-            dma((6,)), dma, dma((3,)), dma, dma((3,)), dma((3,)), dma((3, 2, 3)),
-            dma((3,)), dma((3,)), dma((3,)), dma((3,)), dma, dma,
+            dma((6,)), dma, dma((3,)), dma, dma((3,)), dma((3,)), dma((3, 3, 3)),
+            dma((3,)), dma((3,)), dma((2,)), dma((2,)), dma, dma, dma, dma,
         ],
         compiler_params=pltpu.CompilerParams(
             collective_id=0, has_side_effects=True, vmem_limit_bytes=56 << 20

time: 52.2 us -> 49 us (0.939)
  Pallas kernels: 50.4 us -> 47.1 us
    pallas_call x1, Pallas kernels: 50.4 us -> 47.1 us  [shards(): pl.pallas_call(kernel, out_shape=jax.ShapeDtypeStruct((32, 32, W), BF16),...]
where the time goes in v3:
time: 49 us; the launch traced here: 48.8 us
  Pallas kernels  47.1 us (96%)
  local copies, waits for them, and re-layouts  1.67 us (3%)
    pallas_call x1, Pallas kernels, shards(): pl.pallas_call(kernel, out_shape=jax.ShapeDtypeStruct((32, 32, W), BF16),...  47.1 us
    unnamed x1, local copies, waits for them, and re-layouts  1.67 us

profile of v3, /device:TPU:1, one launch (start us, length us, event | category | flops | bytes accessed | tf_op | source)
XLA Modules:
  0.0 48.8 jit_solution(14486372097021654390)
XLA Ops:
  0.0 47.1 %shard_map.82 = bf16[32,32,128]{2,1,0:T(8,128)(2,1)} custom-call(bf16[64,4096]{1,0:T(8,128)(2,1)} %patches_ref.1, s32[2,64]{1,0:T(2,128)} %bitcast.2, s32[2,64]{1,0:T(2,128)} %bitcast.3, bf16[9,64,64]{2,1,0:T(8,128)(2,1)} %wf_ref.1, bf16[9,128,128]{2,1,0:T(8,128)(2,1)} %wd_ref.1, bf16[9,128,256]{2,1,0:T(8,128)(2,1)} %wp_ref.1, bf16[9,128,384]{2,1,0:T(8,128)(2,1)} %wm_ref.1, ...), custom_call_target="tpu_custom_call" | custom-call | tf_op jit(solution)/shard_map/pallas_call | solution.py:453
  47.1 1.7 %copy.10 = bf16[32,32,128]{2,1,0:T(8,128)(2,1)} copy(bf16[32,32,128]{2,1,0:T(8,128)(2,1)} %shard_map.82) | data formatting | bytes 524288

commit v4 on v3

--- a/solution.py
+++ b/solution.py
@@ -60,7 +60,7 @@
     gathered, slots_out, slots_in, sums_out, sums_in, sums_own, tables_out, tables_in, codes_out, codes_in,
     wf_raw, wd_raw, wp_raw, wm_raw, wo_raw,
     wf, wd, wp, wm, wo,
-    select, place, grid_f, tile, halo, im1, im2, imd, im4, out_f, out_b,
+    select, place, grid_f, tile, halo, im1, im2, imd, im4, out_b,
     load, t_send, t_recv, c_send, c_recv, route_send, route_recv,
     w_send, w_recv, x_send, x_recv, h_send, h_recv, o_send, o_recv,
 ):
@@ -87,13 +87,11 @@
             greet(along(axis, step))
     greet((r, other))
 
+    encoder = [(wf_ref, wf_raw.at[c]), (wd_ref, wd_raw.at[c]), (wp_ref, wp_raw.at[c])]
     loads = [
         pltpu.make_async_copy(src, dst, load.at[n])
         for n, (src, dst) in enumerate(
-            [
-                (patches_ref, gathered.at[0]), (wf_ref, wf_raw), (wd_ref, wd_raw),
-                (wp_ref, wp_raw), (wm_ref, wm_raw), (wo_ref, wo_raw),
-            ]
+            [(patches_ref, gathered.at[0])] + encoder + [(wm_ref, wm_raw), (wo_ref, wo_raw)]
         )
     ]
     for copy in loads:
@@ -142,25 +140,28 @@
     for h in range(3):
         spread_out(0, h, lambda step: gathered.at[0], gathered)
 
-    for copy in loads[1:]:
-        copy.wait()
-    first_rows = pl.ds(pl.multiple_of(64 * c, 64), 64)
-    second_rows = pl.ds(pl.multiple_of(128 * c, 128), 128)
-    wf[first_rows, :] = jnp.concatenate([wf_raw[k] for k in range(9)], axis=1)
-    for k in range(9):
-        wd[second_rows, 128 * k : 128 * k + 128] = wd_raw[k]
-        wp[second_rows, 256 * k : 256 * k + 256] = wp_raw[k]
     weight_copies = [
-        remote(buf.at[rows], buf.at[rows], w_send.at[n], w_recv.at[n], (r, other))
-        for n, (buf, rows) in enumerate([(wf, first_rows), (wd, second_rows), (wp, second_rows)])
+        remote(src, dst, w_send.at[n], w_recv.at[n], (r, other)) for n, (src, dst) in enumerate(encoder)
     ]
     for copy in weight_copies:
         copy.start()
-    for k in range(9):
+    for copy in loads[1:]:
+        copy.wait()
+    for copy in weight_copies:
+        copy.wait_recv()
+    taps_from = [k + other * (6 - 6 * (k // 3)) for k in range(9)]
+    for core in range(2):
+        wf[64 * core : 64 * core + 64, :] = jnp.concatenate(
+            [wf_raw[core, k] for k in taps_from], axis=1
+        )
+    for k, source in enumerate(taps_from):
         i, j = k // 3, k % 3
-        wm[:, 1152 * i + 128 * j : 1152 * i + 128 * j + 128] = wm_raw[k, :, :C1]
-        wm[:, 1152 * i + 384 + 256 * j : 1152 * i + 384 + 256 * j + 256] = wm_raw[k, :, C1:]
-        wo[:, 128 * k : 128 * k + 128] = wo_raw[k]
+        for core in range(2):
+            wd[128 * core : 128 * core + 128, 128 * k : 128 * k + 128] = wd_raw[core, source]
+            wp[128 * core : 128 * core + 128, 256 * k : 256 * k + 256] = wp_raw[core, source]
+        wm[:, 1152 * i + 128 * j : 1152 * i + 128 * j + 128] = wm_raw[source, :, :C1]
+        wm[:, 1152 * i + 384 + 256 * j : 1152 * i + 384 + 256 * j + 256] = wm_raw[source, :, C1:]
+        wo[:, 128 * k : 128 * k + 128] = wo_raw[source]
 
     lane = iota((8, W), 1)
     left = lane < 64
@@ -237,10 +238,12 @@
                 sums_out[:, :, n:e] = sums[32:].astype(BF16).reshape(3, 32, e - n)
         spread_out(2, h, lambda step: sums_out.at[step - 1], sums_in)
 
-    top = jnp.logical_and(r == 0, c == 0)
-    bottom = jnp.logical_and(r == 63, c == 1)
-    keep_top = jnp.where(top, 0.0, 1.0)
-    keep_bottom = jnp.where(bottom, 0.0, 1.0)
+    border = jnp.logical_or(jnp.logical_and(r == 0, c == 0), jnp.logical_and(r == 63, c == 1))
+    keep = jnp.where(border, 0.0, 1.0)
+
+    def tile_row(v):
+        return (15 - v) * other + (16 + v) * c
+
     even = iota((C2, W), 1) % 2 == 0
 
     def taps(x):
@@ -253,18 +256,23 @@
         copy.start()
         return copy
 
-    own_rows = tile.at[pl.ds(10 * c, 22)]
-    own_im1 = im1.at[pl.ds(6 * other, 22)]
+    def halo_copies(e, core):
+        rows = pl.ds(pl.multiple_of(32 * core + 16 * e, 16), 16)
+        for to in range(2):
+            yield remote(
+                tile.at[pl.ds(26 * (1 - to), 6), rows], halo.at[:, rows],
+                h_send.at[e, to], h_recv.at[e, core], ((r + 1 + 62 * to) % 64, to),
+            )
+
+    def send_halo(e):
+        for copy in halo_copies(e, c):
+            copy.start()
 
     def widen(e, core):
-        source = own_rows.at[:, pl.ds(pl.multiple_of(32 * core + 16 * e, 16), 16)]
-        target = [
-            own_im1.at[:, pl.ds(pl.multiple_of(C0 * j + 32 * core + 16 * e, 16), 16)]
-            for j in range(3)
-        ]
+        channels = pl.multiple_of(32 * core + 16 * e, 16)
         for l in range(22):
-            for j, tap in enumerate(taps(source[l])):
-                target[j][l] = tap
+            for j, tap in enumerate(taps(tile[tile_row(l - 6), pl.ds(channels, 16), :])):
+                im1[l, pl.ds(C0 * j + channels, 16), :] = tap
 
     tile_copies = []
     for h in range(3):
@@ -281,75 +289,68 @@
         if h != 1:
             e = h // 2
             tile_copies.append(settle(e))
+            if e == 1:
+                send_halo(e)
             widen(e, c)
             tile_copies[e].wait_recv()
-            if e == 1:
-                halo_copy = remote(
-                    tile.at[pl.ds(26 * other, 6)], halo, h_send, h_recv, ((r + 1 + 62 * c) % 64, c)
-                )
-                halo_copy.start()
+            if e == 0:
+                send_halo(e)
             widen(e, other)
-    for copy in weight_copies:
-        copy.wait_recv()
-
-    def first_rows_of(base, n, source, target):
+
+    def first_rows_of(n):
         f = 4 * n
         window = jnp.concatenate(
-            [source[f + t : f + t + 3].reshape(576, W) for t in range(4)], axis=1
+            [im1[f + t : f + t + 3].reshape(576, W) for t in range(4)], axis=1
         )
         total = jnp.dot(wf[...], window, preferred_element_type=F32)
         for t in range(4):
-            at_row = base + f + t
-            factor = jnp.where(at_row < 5, keep_top, jnp.where(at_row >= 21, keep_bottom, 1.0))
-            row = (silu(total[:, W * t : W * t + W]) * factor).astype(BF16)
-            for j, tap in enumerate(taps(row)):
-                target[f + t, C1 * j : C1 * j + C1] = tap
-
-    def spread_pair(target, at_pair, x):
+            row = silu(total[:, W * t : W * t + W])
+            if f + t >= 21:
+                row = row * keep
+            for j, tap in enumerate(taps(row.astype(BF16))):
+                im2[f + t, C1 * j : C1 * j + C1] = tap
+
+    def spread_pair(at_pair, x):
         for j, tap in enumerate((shift(x, -2), x, shift(x, 2))):
-            target[at_pair, C2 * j : C2 * j + C2] = tap
-
-    def second_pair(base, m, source, target):
+            imd[at_pair, C2 * j : C2 * j + C2] = tap
+
+    def second_pair(m):
         window = jnp.concatenate(
             [
-                jnp.concatenate([source[4 * m + 2 * t + i, 0:384] for i in range(3)], axis=0)
+                jnp.concatenate([im2[4 * m + 2 * t + i + other, 0:384] for i in range(3)], axis=0)
                 for t in range(2)
             ],
             axis=1,
         )
         total = jnp.dot(wd[...], window, preferred_element_type=F32)
         pair = silu(jnp.where(even, total[:, :W], pltpu.roll(total[:, W:], 1, 1)))
-        at_pair = base + m
-        factor = jnp.where(at_pair == 0, keep_top, jnp.where(at_pair == 5, keep_bottom, 1.0))
-        spread_pair(target, 2 * m, (pair * factor).astype(BF16))
-
-    def blend(m, target):
-        a, b = target[2 * m, C2 : 2 * C2], target[2 * m + 2, C2 : 2 * C2]
-        spread_pair(target, 2 * m + 1, jnp.where(even, shift(a, 1), shift(b, -1)))
-
-    def third_pairs(base, ms, source, target):
-        window = jnp.concatenate(
-            [source[2 * m : 2 * m + 3].reshape(2304, W) for m in ms], axis=1
-        )
+        if m == 5:
+            pair = pair * keep
+        spread_pair(2 * m, pair.astype(BF16))
+
+    def blend(m):
+        a, b = imd[2 * m, C2 : 2 * C2], imd[2 * m + 2, C2 : 2 * C2]
+        spread_pair(2 * m + 1, jnp.where(even, shift(a, 1), shift(b, -1)))
+
+    def third_pairs(ms):
+        window = jnp.concatenate([imd[2 * m : 2 * m + 3].reshape(2304, W) for m in ms], axis=1)
         total = jnp.dot(wp[...], window, preferred_element_type=F32)
         for t, m in enumerate(ms):
-            third = silu(total[:, W * t : W * t + W]) + source[2 * m + 1, C2 : 2 * C2].astype(F32)
-            factor = jnp.where(
-                even,
-                jnp.where(base + m == 0, keep_top, 1.0),
-                jnp.where(base + m == 4, keep_bottom, 1.0),
-            )
-            third = (third * factor).astype(BF16)
+            third = silu(total[:, W * t : W * t + W]) + imd[2 * m + 1, C2 : 2 * C2].astype(F32)
+            if m == 4:
+                third = jnp.where(even, third, third * keep)
+            third = third.astype(BF16)
             l1, l2, r1, r2 = shift(third, -1), shift(third, -2), shift(third, 1), shift(third, 2)
             lane = iota((C2, W), 1)
+            zero = jnp.zeros_like(third)
             ups = (
                 (
                     jnp.where(even, l2, l1),
                     jnp.where(even, third, l1),
-                    jnp.where(lane == W - 1, jnp.zeros_like(third), jnp.where(even, third, r1)),
+                    jnp.where(lane == W - 1, zero, jnp.where(even, third, r1)),
                 ),
                 (
-                    jnp.where(lane == 0, jnp.zeros_like(third), jnp.where(even, l1, third)),
+                    jnp.where(lane == 0, zero, jnp.where(even, l1, third)),
                     jnp.where(even, r1, third),
                     jnp.where(even, r1, r2),
                 ),
@@ -357,84 +358,69 @@
             for half in range(2):
                 for j in range(3):
                     f = 4 * m + 3 + 2 * half
-                    target[f, 384 + C2 * j : 384 + C2 * j + C2] = ups[half][j]
-                    target[f + 1, 384 + C2 * j : 384 + C2 * j + C2] = ups[half][j]
-
-    def fourth_rows(base, n, source, target):
+                    im2[f, 384 + C2 * j : 384 + C2 * j + C2] = ups[half][j]
+                    im2[f + 1, 384 + C2 * j : 384 + C2 * j + C2] = ups[half][j]
+
+    def fourth_rows(n):
         g = 2 * n
         window = jnp.concatenate(
-            [source[g + 3 + t : g + 6 + t].reshape(3456, W) for t in range(2)], axis=1
+            [im2[g + 3 + t : g + 6 + t].reshape(3456, W) for t in range(2)], axis=1
         )
         total = jnp.dot(wm[...], window, preferred_element_type=F32)
         for t in range(2):
-            at_row = base + g + t
-            factor = jnp.where(at_row < 1, keep_top, jnp.where(at_row >= 17, keep_bottom, 1.0))
-            row = (silu(total[:, W * t : W * t + W]) * factor).astype(BF16)
-            for j, tap in enumerate(taps(row)):
-                target[g + t, C1 * j : C1 * j + C1] = tap
-
-    def out_rows(n, source, skip, target):
+            row = silu(total[:, W * t : W * t + W])
+            if g + t == 17:
+                row = row * keep
+            for j, tap in enumerate(taps(row.astype(BF16))):
+                im4[g + t, C1 * j : C1 * j + C1] = tap
+
+    def out_rows(n):
         f = 4 * n
         window = jnp.concatenate(
-            [source[f + t : f + t + 3].reshape(1152, W) for t in range(4)], axis=1
+            [im4[f + t : f + t + 3].reshape(1152, W) for t in range(4)], axis=1
         )
         total = jnp.dot(wo[...], window, preferred_element_type=F32)
         for t in range(4):
-            row = total[:, W * t : W * t + W] + skip[f + t].astype(F32)
-            target[pl.ds(f + t, C0, stride=8), :] = row
-
-    base = 8 * other
-    at_first, at_im2 = im1.at[pl.ds(base, 22)], im2.at[pl.ds(base, 20)]
-    at_imd, at_im4 = imd.at[pl.ds(4 * other, 7)], im4.at[pl.ds(base, 10)]
+            at_row = tile_row(f + t)
+            row = total[:, W * t : W * t + W] + tile[at_row].astype(F32)
+            out_b[f + t] = row.astype(BF16)
+            remote(
+                out_b.at[f + t, pl.ds(pl.multiple_of(32 * other, 32), 32)], out_ref.at[at_row],
+                o_send, o_recv, (r, other),
+            ).start()
+            out_ref[at_row] = out_b[f + t, pl.ds(pl.multiple_of(32 * c, 32), 32), :]
+
     for n in range(5):
-        first_rows_of(base, n, at_first, at_im2)
+        first_rows_of(n)
     for m in range(4):
-        second_pair(2 * other, m, at_im2, at_imd)
+        second_pair(m)
     for m in range(3):
-        blend(m, at_imd)
-    third_pairs(2 * other, [0, 1], at_imd, at_im2)
-    third_pairs(2 * other, [2], at_imd, at_im2)
-    for n in range(5):
-        fourth_rows(base, n, at_im2, at_im4)
-    for n in range(2):
-        out_rows(n, at_im4, tile.at[pl.ds(8 + 8 * c, 8)], out_f.at[other])
-    halo_copy.wait_recv()
-
-    @pl.when(jnp.logical_or(top, bottom))
+        blend(m)
+    third_pairs([0, 1])
+    third_pairs([2])
+    for e in range(2):
+        for core in range(2):
+            next(halo_copies(e, core)).wait_recv()
+
+    @pl.when(border)
     def _():
         halo[...] = jnp.zeros((6, C0, W), BF16)
 
-    at_first, at_im2 = im1.at[pl.ds(22 * c, 6)], im2.at[pl.ds(20 * c, 8)]
     for l in range(6):
-        for j, tap in enumerate(taps(halo[l])):
-            at_first[l, C0 * j : C0 * j + C0] = tap
-    at_first = im1.at[pl.ds(20 * c, 10)]
-    for n in range(2):
-        first_rows_of(20 * c, n, at_first, at_im2)
-    at_im2, at_imd = im2.at[pl.ds(16 * c, 9)], imd.at[pl.ds(8 * c, 3)]
-    for m in range(2):
-        second_pair(4 * c, m, at_im2, at_imd)
-    at_im2, at_imd = im2.at[pl.ds(12 * c, 11)], imd.at[pl.ds(6 * c, 5)]
-    for m in range(2):
-        blend(m, at_imd)
-    third_pairs(3 * c, [0, 1], at_imd, at_im2)
-    at_im2, at_im4 = im2.at[pl.ds(10 * c, 13)], im4.at[pl.ds(10 * c, 8)]
+        for j, tap in enumerate(taps(halo[(5 - l) * other + l * c])):
+            im1[22 + l, C0 * j : C0 * j + C0] = tap
+    for n in range(5, 7):
+        first_rows_of(n)
+    for m in range(4, 6):
+        second_pair(m)
+    for m in range(3, 5):
+        blend(m)
+    third_pairs([3, 4])
+    for n in range(9):
+        fourth_rows(n)
     for n in range(4):
-        fourth_rows(10 * c, n, at_im2, at_im4)
-    at_im4 = im4.at[pl.ds(8 * c, 10)]
-    for n in range(2):
-        out_rows(n, at_im4, tile.at[pl.ds(24 * c, 8)], out_f.at[c])
-    out_b[...] = jnp.concatenate(
-        [out_f[n].reshape(C0, 8, W) for n in range(2)], axis=1
-    ).astype(BF16)
-    mine = pl.ds(pl.multiple_of(HALF * c, HALF), HALF)
-    out_copy = remote(
-        out_b.at[pl.ds(32 * other, 32)], out_ref.at[:, mine, :], o_send, o_recv, (r, other)
-    )
-    out_copy.start()
-    out_ref[:, mine, :] = out_b[pl.ds(32 * c, 32)]
-
-    for copy in weight_copies + tile_copies + [halo_copy]:
+        out_rows(n)
+    for copy in weight_copies + tile_copies + [*halo_copies(0, c), *halo_copies(1, c)]:
         copy.wait_send()
     for phase, buffer in enumerate((gathered, slots_in, sums_in)):
         whole = buffer.at[pl.ds(1, 3)]
@@ -443,14 +429,15 @@
     remote(three, three, t_send, o_recv, (r, other)).wait_send()
     three = codes_in.at[:, pl.ds(1, 3)]
     remote(three, three, c_send, o_recv, (r, other)).wait_send()
-    out_copy.wait()
+    rows = out_ref.at[pl.ds(0, HALF)]
+    remote(rows, rows, o_send, o_recv, (r, other)).wait()
 
 
 def shards(patches, region, cell, *weights):
     vmem = pl.BlockSpec(memory_space=pltpu.VMEM)
     anywhere = pl.BlockSpec(memory_space=pl.ANY)
     dma = pltpu.SemaphoreType.DMA
-    return pl.pallas_call(
+    rows = pl.pallas_call(
         kernel,
         out_shape=jax.ShapeDtypeStruct((32, 32, W), BF16),
         in_specs=[anywhere, vmem, vmem] + [anywhere] * 5,
@@ -466,9 +453,9 @@
             pltpu.VMEM((3, 4, 8, W), F32),
             pltpu.VMEM((3, 4, 8, W), F32),
             pltpu.VMEM((3, 4, 8, W), F32),
-            pltpu.VMEM((9, 64, C0), BF16),
-            pltpu.VMEM((9, 128, C1), BF16),
-            pltpu.VMEM((9, 128, C2), BF16),
+            pltpu.VMEM((2, 9, 64, C0), BF16),
+            pltpu.VMEM((2, 9, 128, C1), BF16),
+            pltpu.VMEM((2, 9, 128, C2), BF16),
             pltpu.VMEM((9, C1, C1 + C2), BF16),
             pltpu.VMEM((9, C0, C1), BF16),
             pltpu.VMEM((C1, 9 * C0), BF16),
@@ -485,15 +472,15 @@
             pltpu.VMEM((28, 3 * (C1 + C2), W), BF16),
             pltpu.VMEM((11, 3 * C2, W), BF16),
             pltpu.VMEM((18, 3 * C1, W), BF16),
-            pltpu.VMEM((2, C0 * 8, W), F32),
-            pltpu.VMEM((C0, HALF, W), BF16),
+            pltpu.VMEM((HALF, C0, W), BF16),
             dma((6,)), dma, dma((3,)), dma, dma((3,)), dma((3,)), dma((3, 3, 3)),
-            dma((3,)), dma((3,)), dma((2,)), dma((2,)), dma, dma, dma, dma,
+            dma((3,)), dma((3,)), dma((2,)), dma((2,)), dma((2, 2)), dma((2, 2)), dma, dma,
         ],
         compiler_params=pltpu.CompilerParams(
             collective_id=0, has_side_effects=True, vmem_limit_bytes=56 << 20
         ),
     )(patches, region.T, cell.T, *weights)
+    return jnp.transpose(rows, (1, 0, 2))
 
 
 def solution(mesh):

time: 49 us -> 47 us (0.959)
  Pallas kernels: 47.1 us -> 45 us
    pallas_call x1, Pallas kernels: 47.1 us -> 45 us  [shards(): pl.pallas_call(kernel, out_shape=jax.ShapeDtypeStruct((32, 32, W), BF16),...]
    transpose x0 -> x1, local copies, waits for them, and re-layouts: none -> 1.76 us  [shards(): return jnp.transpose(rows, (1, 0, 2))]
    unnamed x1 -> x0, local copies, waits for them, and re-layouts: 1.67 us -> none
where the time goes in v4:
time: 47 us; the launch traced here: 46.8 us
  Pallas kernels  45 us (96%)
  local copies, waits for them, and re-layouts  1.76 us (4%)
    pallas_call x1, Pallas kernels, shards(): pl.pallas_call(kernel, out_shape=jax.ShapeDtypeStruct((32, 32, W), BF16),...  45 us
    transpose x1, local copies, waits for them, and re-layouts, shards(): return jnp.transpose(rows, (1, 0, 2))  1.76 us

profile of v4, /device:TPU:1, one launch (start us, length us, event | category | flops | bytes accessed | tf_op | source)
XLA Modules:
  0.0 46.8 jit_solution(14782527923244827454)
XLA Ops:
  0.0 45.0 %shard_map.82 = bf16[32,32,128]{2,1,0:T(8,128)(2,1)} custom-call(bf16[64,4096]{1,0:T(8,128)(2,1)} %patches_ref.1, s32[2,64]{1,0:T(2,128)} %bitcast.4, s32[2,64]{1,0:T(2,128)} %bitcast.5, bf16[9,64,64]{2,1,0:T(8,128)(2,1)} %wf_ref.1, bf16[9,128,128]{2,1,0:T(8,128)(2,1)} %wd_ref.1, bf16[9,128,256]{2,1,0:T(8,128)(2,1)} %wp_ref.1, bf16[9,128,384]{2,1,0:T(8,128)(2,1)} %wm_ref.1, ...), custom_call_target="tpu_custom_call" | custom-call | tf_op jit(solution)/shard_map/pallas_call | solution.py:440
  45.0 1.8 %copy.9 = bf16[32,32,128]{2,1,0:T(8,128)(2,1)} copy(bf16[32,32,128]{2,0,1:T(8,128)(2,1)} %bitcast.3) | data formatting | bytes 524288 | tf_op jit(solution)/shard_map/transpose | solution.py:483

commit v5 on v4

--- a/solution.py
+++ b/solution.py
@@ -62,7 +62,7 @@
     wf, wd, wp, wm, wo,
     select, place, grid_f, tile, halo, im1, im2, imd, im4, out_b,
     load, t_send, t_recv, c_send, c_recv, route_send, route_recv,
-    w_send, w_recv, x_send, x_recv, h_send, h_recv, o_send, o_recv,
+    w_send, w_recv, x_send, x_recv, h_send, h_recv, o_send, o_recv, o_own,
 ):
     r, c = lax.axis_index("region"), lax.axis_index("chan")
     at = (r // 16, (r // 4) % 4, r % 4)
@@ -157,11 +157,20 @@
     for k, source in enumerate(taps_from):
         i, j = k // 3, k % 3
         for core in range(2):
-            wd[128 * core : 128 * core + 128, 128 * k : 128 * k + 128] = wd_raw[core, source]
             wp[128 * core : 128 * core + 128, 256 * k : 256 * k + 256] = wp_raw[core, source]
         wm[:, 1152 * i + 128 * j : 1152 * i + 128 * j + 128] = wm_raw[source, :, :C1]
         wm[:, 1152 * i + 384 + 256 * j : 1152 * i + 384 + 256 * j + 256] = wm_raw[source, :, C1:]
         wo[:, 128 * k : 128 * k + 128] = wo_raw[source]
+
+    for k in range(12):
+        i, j = k // 3, k % 3
+        source = 3 * (min(3 - i, 2) * other + min(i, 2) * c) + j
+        used = (c == 1 if i == 0 else c == 0) if i in (0, 3) else None
+        for core in range(2):
+            value = wd_raw[core, source]
+            if used is not None:
+                value = jnp.where(used, value, jnp.zeros_like(value))
+            wd[128 * core : 128 * core + 128, 128 * k : 128 * k + 128] = value
 
     lane = iota((8, W), 1)
     left = lane < 64
@@ -317,7 +326,7 @@
     def second_pair(m):
         window = jnp.concatenate(
             [
-                jnp.concatenate([im2[4 * m + 2 * t + i + other, 0:384] for i in range(3)], axis=0)
+                jnp.concatenate([im2[4 * m + 2 * t + i, 0:384] for i in range(4)], axis=0)
                 for t in range(2)
             ],
             axis=1,
@@ -381,22 +390,25 @@
         )
         total = jnp.dot(wo[...], window, preferred_element_type=F32)
         for t in range(4):
-            at_row = tile_row(f + t)
-            row = total[:, W * t : W * t + W] + tile[at_row].astype(F32)
-            out_b[f + t] = row.astype(BF16)
-            remote(
-                out_b.at[f + t, pl.ds(pl.multiple_of(32 * other, 32), 32)], out_ref.at[at_row],
-                o_send, o_recv, (r, other),
-            ).start()
-            out_ref[at_row] = out_b[f + t, pl.ds(pl.multiple_of(32 * c, 32), 32), :]
+            row = total[:, W * t : W * t + W] + tile[tile_row(f + t)].astype(F32)
+            out_b[(15 - f - t) * other + (f + t) * c] = row.astype(BF16)
+        start = (12 - f) * other + f * c
+        source, target = out_b.at[pl.ds(start, 4)], out_ref.at[pl.ds(HALF * c + start, 4)]
+        remote(
+            source.at[:, pl.ds(pl.multiple_of(32 * other, 32), 32)], target, o_send, o_recv, (r, other)
+        ).start()
+        pltpu.make_async_copy(
+            source.at[:, pl.ds(pl.multiple_of(32 * c, 32), 32)], target, o_own
+        ).start()
 
     for n in range(5):
         first_rows_of(n)
-    for m in range(4):
-        second_pair(m)
-    for m in range(3):
-        blend(m)
-    third_pairs([0, 1])
+        if n:
+            second_pair(n - 1)
+        if n > 1:
+            blend(n - 2)
+        if n == 3:
+            third_pairs([0, 1])
     third_pairs([2])
     for e in range(2):
         for core in range(2):
@@ -431,6 +443,7 @@
     remote(three, three, c_send, o_recv, (r, other)).wait_send()
     rows = out_ref.at[pl.ds(0, HALF)]
     remote(rows, rows, o_send, o_recv, (r, other)).wait()
+    pltpu.make_async_copy(rows, rows, o_own).wait()
 
 
 def shards(patches, region, cell, *weights):
@@ -441,7 +454,7 @@
         kernel,
         out_shape=jax.ShapeDtypeStruct((32, 32, W), BF16),
         in_specs=[anywhere, vmem, vmem] + [anywhere] * 5,
-        out_specs=vmem,
+        out_specs=anywhere,
         scratch_shapes=[
             pltpu.VMEM((4, 64, 4096), BF16),
             pltpu.VMEM((3, 64, 4096), BF16),
@@ -459,7 +472,7 @@
             pltpu.VMEM((9, C1, C1 + C2), BF16),
             pltpu.VMEM((9, C0, C1), BF16),
             pltpu.VMEM((C1, 9 * C0), BF16),
-            pltpu.VMEM((C2, 9 * C1), BF16),
+            pltpu.VMEM((C2, 12 * C1), BF16),
             pltpu.VMEM((C2, 9 * C2), BF16),
             pltpu.VMEM((C1, 9 * (C1 + C2)), BF16),
             pltpu.VMEM((C0, 9 * C1), BF16),
@@ -474,7 +487,7 @@
             pltpu.VMEM((18, 3 * C1, W), BF16),
             pltpu.VMEM((HALF, C0, W), BF16),
             dma((6,)), dma, dma((3,)), dma, dma((3,)), dma((3,)), dma((3, 3, 3)),
-            dma((3,)), dma((3,)), dma((2,)), dma((2,)), dma((2, 2)), dma((2, 2)), dma, dma,
+            dma((3,)), dma((3,)), dma((2,)), dma((2,)), dma((2, 2)), dma((2, 2)), dma, dma, dma,
         ],
         compiler_params=pltpu.CompilerParams(
             collective_id=0, has_side_effects=True, vmem_limit_bytes=56 << 20

time: 47 us -> 46.2 us (0.983)
  Pallas kernels: 45 us -> 44.3 us
    pallas_call x1, Pallas kernels: 45 us -> 44.3 us  [shards(): pl.pallas_call(kernel, out_shape=jax.ShapeDtypeStruct((32, 32, W), BF16),...]
where the time goes in v5:
time: 46.2 us; the launch traced here: 46.1 us
  Pallas kernels  44.3 us (96%)
  local copies, waits for them, and re-layouts  1.76 us (4%)
    pallas_call x1, Pallas kernels, shards(): pl.pallas_call(kernel, out_shape=jax.ShapeDtypeStruct((32, 32, W), BF16),...  44.3 us
    transpose x1, local copies, waits for them, and re-layouts, shards(): return jnp.transpose(rows, (1, 0, 2))  1.76 us

profile of v5, /device:TPU:1, one launch (start us, length us, event | category | flops | bytes accessed | tf_op | source)
XLA Modules:
  0.0 46.1 jit_solution(8896841373102090530)
XLA Ops:
  0.0 44.3 %shard_map.82 = bf16[32,32,128]{2,1,0:T(8,128)(2,1)} custom-call(bf16[64,4096]{1,0:T(8,128)(2,1)} %patches_ref.1, s32[2,64]{1,0:T(2,128)} %bitcast.4, s32[2,64]{1,0:T(2,128)} %bitcast.5, bf16[9,64,64]{2,1,0:T(8,128)(2,1)} %wf_ref.1, bf16[9,128,128]{2,1,0:T(8,128)(2,1)} %wd_ref.1, bf16[9,128,256]{2,1,0:T(8,128)(2,1)} %wp_ref.1, bf16[9,128,384]{2,1,0:T(8,128)(2,1)} %wm_ref.1, ...), custom_call_target="tpu_custom_call" | custom-call | tf_op jit(solution)/shard_map/pallas_call | solution.py:453
  44.3 1.8 %copy.9 = bf16[32,32,128]{2,1,0:T(8,128)(2,1)} copy(bf16[32,32,128]{2,0,1:T(8,128)(2,1)} %bitcast.3) | data formatting | bytes 524288 | tf_op jit(solution)/shard_map/transpose | solution.py:496

commit v6 on v5

--- a/solution.py
+++ b/solution.py
@@ -262,6 +262,8 @@
         mine = pl.ds(pl.multiple_of(32 * c + 16 * e, 16), 16)
         tile[:, mine, :] = grid_f[e].astype(BF16).reshape(32, 16, W)
         copy = remote(tile.at[:, mine], tile.at[:, mine], x_send.at[e], x_recv.at[e], (r, other))
+        if e == 1:
+            send_halo(e)
         copy.start()
         return copy
 
@@ -298,8 +300,6 @@
         if h != 1:
             e = h // 2
             tile_copies.append(settle(e))
-            if e == 1:
-                send_halo(e)
             widen(e, c)
             tile_copies[e].wait_recv()
             if e == 0:
@@ -410,6 +410,8 @@
         if n == 3:
             third_pairs([0, 1])
     third_pairs([2])
+    for n in range(3):
+        fourth_rows(n)
     for e in range(2):
         for core in range(2):
             next(halo_copies(e, core)).wait_recv()
@@ -428,7 +430,7 @@
     for m in range(3, 5):
         blend(m)
     third_pairs([3, 4])
-    for n in range(9):
+    for n in range(3, 9):
         fourth_rows(n)
     for n in range(4):
         out_rows(n)

time: 46.2 us -> 46.4 us (level)
  no operation moved by 1% of the time
where the time goes in v6:
time: 46.4 us; the launch traced here: 46.2 us
  Pallas kernels  44.4 us (96%)
  local copies, waits for them, and re-layouts  1.76 us (4%)
    pallas_call x1, Pallas kernels, shards(): pl.pallas_call(kernel, out_shape=jax.ShapeDtypeStruct((32, 32, W), BF16),...  44.4 us
    transpose x1, local copies, waits for them, and re-layouts, shards(): return jnp.transpose(rows, (1, 0, 2))  1.76 us

profile of v6, /device:TPU:1, one launch (start us, length us, event | category | flops | bytes accessed | tf_op | source)
XLA Modules:
  0.0 46.2 jit_solution(13707050539542675587)
XLA Ops:
  0.0 44.4 %shard_map.82 = bf16[32,32,128]{2,1,0:T(8,128)(2,1)} custom-call(bf16[64,4096]{1,0:T(8,128)(2,1)} %patches_ref.1, s32[2,64]{1,0:T(2,128)} %bitcast.4, s32[2,64]{1,0:T(2,128)} %bitcast.5, bf16[9,64,64]{2,1,0:T(8,128)(2,1)} %wf_ref.1, bf16[9,128,128]{2,1,0:T(8,128)(2,1)} %wd_ref.1, bf16[9,128,256]{2,1,0:T(8,128)(2,1)} %wp_ref.1, bf16[9,128,384]{2,1,0:T(8,128)(2,1)} %wm_ref.1, ...), custom_call_target="tpu_custom_call" | custom-call | tf_op jit(solution)/shard_map/pallas_call | solution.py:455
  44.4 1.8 %copy.9 = bf16[32,32,128]{2,1,0:T(8,128)(2,1)} copy(bf16[32,32,128]{2,0,1:T(8,128)(2,1)} %bitcast.3) | data formatting | bytes 524288 | tf_op jit(solution)/shard_map/transpose | solution.py:498
